TPU v7x, 32 devices: a whole 2x2x4 slice. The times are simulated.
32 devices in a mesh: segment: 4 (over y, core), dp: 8 (over z, x).
Axes of the slice: x: 2, y: 2, z: 4, core: 2. Of those that a mesh axis runs over, the one named last changes fastest.
Arguments:
- student_in: bfloat16 [4, 16, 8, 8, 512], P(None, 'dp'), may hold values from -6 to 6
- teacher_in: bfloat16 [4, 16, 8, 8, 512], P(None, 'dp'), may hold values from -6 to 6
- out_grad: bfloat16 [4, 16, 8, 8, 512], P(None, 'dp'), may hold values from -6 to 6
- student_params: float32 [4, 2621440], P('segment', 'dp'), may hold values from -0.5625 to 0.5625, as said below
- teacher_params: float32 [4, 2621440], P('segment', 'dp'), may hold values from -0.5625 to 0.5625, as said below
Outputs:
- teacher_acts: bfloat16 [4, 4, 16, 8, 8, 512], P('segment', None, 'dp')
- input_grads: bfloat16 [4, 4, 16, 8, 8, 512], P('segment', None, 'dp')
- param_grads: float32 [4, 2621440], P('segment', 'dp')
- teacher_new: float32 [4, 2621440], P('segment', 'dp')
Inputs may be any that keep to these rules, and one draw needn't show every extreme that they name: `student_params`: independent entries of both signs. `teacher_params`: independent entries of both signs.
All inputs are finite; a program needn't handle non-finite values.
Results may differ from a plain program's by a relative error of at most 0.03.
Values may be sent and summed in bfloat16 or wider, within the bound.
A program may use at most 128 MiB of HBM per device.

v0:
```python
import jax
import jax.numpy as jnp
from jax import lax
from jax.sharding import PartitionSpec as P

SE = 256


ema_keep = 0.99
step_rate = 0.001


def from_behind(array, axis, by):
    peers = lax.axis_size(axis)
    pairs = [(i, i + by) for i in range(peers) if 0 <= i + by < peers]
    return lax.ppermute(array, axis, pairs)


def split_row(row, channels, squeeze):
    tap_count = 9 * channels * channels
    kernel = row[:tap_count].reshape(9 * channels, channels)
    reduce_w = row[tap_count : tap_count + channels * squeeze].reshape(channels, squeeze)
    expand_w = row[tap_count + channels * squeeze :].reshape(squeeze, channels)
    return (kernel, reduce_w, expand_w)


def gated_block(images, kernel, reduce_w, expand_w):
    side_h, side_w, channels = (images.shape[1], images.shape[2], images.shape[3])
    padded = jnp.pad(images, ((0, 0), (1, 1), (1, 1), (0, 0)))
    columns = jnp.concatenate(
        [
            padded[:, row_off : row_off + side_h, col_off : col_off + side_w, :]
            for row_off in range(3)
            for col_off in range(3)
        ],
        axis=-1,
    )
    mixed_sum = jnp.dot(
        columns.reshape(-1, 9 * channels), kernel, preferred_element_type=jnp.float32
    )
    active = jax.nn.silu(mixed_sum).reshape(images.shape)
    pooled = jnp.mean(active, axis=(1, 2)).astype(jnp.bfloat16)
    hidden = jax.nn.silu(jnp.dot(pooled, reduce_w, preferred_element_type=jnp.float32)).astype(
        jnp.bfloat16
    )
    gate_val = jax.nn.sigmoid(jnp.dot(hidden, expand_w, preferred_element_type=jnp.float32))
    return (images.astype(jnp.float32) + active * gate_val[:, None, None, :]).astype(jnp.bfloat16)


def one_image(picture, kernel, reduce_w, expand_w, cotangent):

    def local_block(inputs_one, kern_one, red_one, exp_one):
        return gated_block(inputs_one[None], kern_one, red_one, exp_one)[0]

    _, pull_back = jax.vjp(local_block, picture, kernel, reduce_w, expand_w)
    return pull_back(cotangent)


def per_device(student_in, teacher_in, out_grad, student_params, teacher_params):
    channels = student_in.shape[-1]
    micro_count = student_in.shape[0]
    sections = lax.axis_size("segment")
    section = lax.axis_index("segment")
    step_count = micro_count + sections - 1
    is_first = section == 0
    is_last = section == sections - 1
    student_row = lax.all_gather(student_params.astype(jnp.bfloat16), "dp", axis=1, tiled=True)[0]
    teacher_row = lax.all_gather(teacher_params.astype(jnp.bfloat16), "dp", axis=1, tiled=True)[0]
    student_w = split_row(student_row, channels, SE)
    teacher_w = split_row(teacher_row, channels, SE)
    empty_acts = jnp.zeros(student_in.shape[1:], jnp.bfloat16)
    empty_store = jnp.zeros(student_in.shape, jnp.bfloat16)

    def teacher_part(step_now, received, teacher_out):
        position = step_now - section
        active_step = (position >= 0) & (position < micro_count)
        slot_now = jnp.clip(position, 0, micro_count - 1)
        picture = jnp.where(is_first, teacher_in[slot_now], received)
        result = lax.cond(active_step, lambda: gated_block(picture, *teacher_w), lambda: empty_acts)
        teacher_out = teacher_out.at[slot_now].set(
            jnp.where(active_step, result, teacher_out[slot_now])
        )
        return (result, teacher_out)

    def student_part(step_now, received, saved):
        position = step_now - section
        active_step = (position >= 0) & (position < micro_count)
        slot_now = jnp.clip(position, 0, micro_count - 1)
        picture = jnp.where(is_first, student_in[slot_now], received)
        result = lax.cond(active_step, lambda: gated_block(picture, *student_w), lambda: empty_acts)
        saved = saved.at[slot_now].set(jnp.where(active_step, picture, saved[slot_now]))
        return (result, saved)

    def forward_step(step_now, state_now):
        sent_student, sent_teacher, saved, teacher_out = state_now
        got_student, got_teacher = from_behind((sent_student, sent_teacher), "segment", 1)
        sent_teacher, teacher_out = teacher_part(step_now, got_teacher, teacher_out)
        sent_student, saved = student_part(step_now, got_student, saved)
        return (sent_student, sent_teacher, saved, teacher_out)

    _, _, saved, teacher_out = lax.fori_loop(
        0, step_count, forward_step, (empty_acts, empty_acts, empty_store, empty_store)
    )
    kernel, reduce_w, expand_w = student_w
    zero_sums = (
        jnp.zeros(kernel.shape, jnp.float32),
        jnp.zeros(reduce_w.shape, jnp.float32),
        jnp.zeros(expand_w.shape, jnp.float32),
    )
    zero_shard = jnp.zeros(student_params.shape, jnp.float32)

    def backward_step(step_now, state_now):
        sent_grad, totals, shard_sum, input_grads, sent_teacher, teacher_out = state_now
        got_grad = from_behind(sent_grad, "segment", -1)
        position = step_now - (sections - 1 - section)
        active_step = (position >= 0) & (position < micro_count)
        slot_now = micro_count - 1 - jnp.clip(position, 0, micro_count - 1)
        cotangent = jnp.where(is_last, out_grad[slot_now], got_grad)

        def compute(sums_in):
            d_in, d_kern, d_red, d_exp = jax.vmap(one_image, in_axes=(0, None, None, None, 0))(
                saved[slot_now], kernel, reduce_w, expand_w, cotangent
            )
            return (
                d_in,
                (
                    sums_in[0] + jnp.sum(d_kern.astype(jnp.float32), axis=0),
                    sums_in[1] + jnp.sum(d_red.astype(jnp.float32), axis=0),
                    sums_in[2] + jnp.sum(d_exp.astype(jnp.float32), axis=0),
                ),
            )

        def skip_step(sums_in):
            return (empty_acts, sums_in)

        d_in, totals = lax.cond(active_step, compute, skip_step, totals)
        input_grads = input_grads.at[slot_now].set(
            jnp.where(active_step, d_in, input_grads[slot_now])
        )
        return (d_in, totals, shard_sum, input_grads, sent_teacher, teacher_out)

    _, totals, shard_sum, input_grads, _, teacher_out = lax.fori_loop(
        0,
        step_count,
        backward_step,
        (empty_acts, zero_sums, zero_shard, empty_store, empty_acts, teacher_out),
    )
    grad_shard = lax.psum_scatter(
        jnp.concatenate([totals[0].reshape(-1), totals[1].reshape(-1), totals[2].reshape(-1)])[
            None, :
        ].astype(jnp.bfloat16),
        "dp",
        scatter_dimension=1,
        tiled=True,
    ).astype(jnp.float32)
    teacher_new = ema_keep * teacher_params + (1.0 - ema_keep) * (
        student_params - step_rate * grad_shard
    )
    return (teacher_out[None], input_grads[None], grad_shard, teacher_new)


def solution(mesh):
    placed = (
        P(None, "dp", None, None, None),
        P(None, "dp", None, None, None),
        P(None, "dp", None, None, None),
        P("segment", "dp"),
        P("segment", "dp"),
    )
    return jax.shard_map(
        per_device,
        mesh=mesh,
        in_specs=placed,
        out_specs=(
            P("segment", None, "dp", None, None, None),
            P("segment", None, "dp", None, None, None),
            P("segment", "dp"),
            P("segment", "dp"),
        ),
        check_vma=False,
    )
```

profile of v0, /device:TPU:0, one launch (start us, length us, event | category | flops | bytes accessed | tf_op | source)
XLA Modules:
  0.0 1262.7 jit_solution(3363511186872142740)
XLA Ops:
  14.3 150.2 %all-gather.3.cloned.1.call-done = bf16[1,2621440]{1,0:T(2,128)(2,1)} async-done(((bf16[1,327680]{1,0:T(2,128)(2,1)}), bf16[1,2621440]{1,0:T(2,128)(2,1)}) %all-gather.3.cloned.1.call-update) | async-done | bytes 5242896 | tf_op jit(solution)/shard_map/all_gather | solution.py:67
  164.5 82.1 %slice_reduce_fusion.1 = bf16[2359296]{0:T(1024)(128)(2,1)} fusion(bf16[1,2621440]{1,0:T(2,128)(2,1)} %all-gather.3.cloned.1.call-done), kind=kLoop, calls=%fused_computation.167 | loop fusion | bytes 9437184 | tf_op jit(solution)/shard_map/slice | solution.py:21
  246.6 8.5 reshape.440
  255.1 4.2 slice_reduce_fusion.4
  259.6 56.7 %all-gather.5.cloned.1.call-done = bf16[1,2621440]{1,0:T(2,128)(2,1)} async-done(((bf16[1,327680]{1,0:T(2,128)(2,1)}), bf16[1,2621440]{1,0:T(2,128)(2,1)}) %all-gather.5.cloned.1.call-update) | async-done | bytes 5242896 | tf_op jit(solution)/shard_map/all_gather | solution.py:68
  316.3 82.2 %slice_reduce_fusion = bf16[2359296]{0:T(1024)(128)(2,1)} fusion(bf16[1,2621440]{1,0:T(2,128)(2,1)} %all-gather.5.cloned.1.call-done), kind=kLoop, calls=%fused_computation.166 | loop fusion | bytes 9437184 | tf_op jit(solution)/shard_map/slice | solution.py:21
  398.5 8.5 reshape.443
  407.0 4.2 slice_reduce_fusion.2
  412.9 123.5 %while.45 = (s32[]{:T(128)}, bf16[2,8,8,512]{3,2,1,0:T(8,128)(2,1)}, bf16[2,8,8,512]{3,2,1,0:T(8,128)(2,1)}, bf16[4,2,8,8,512]{4,3,2,1,0:T(8,128)(2,1)S(1)}, bf1...) while((s32[]{:T(128)}, ...), condition=%wide.region_8.9_spmd, body=%wide.region_0.8_spmd.sunk | while | flops 1212167168 | bytes 22184476 | solution.py:101
  414.3 4.1 collective-permute-start.1
  420.8 4.6 conditional.6
  425.4 5.5 conditional.7
  437.5 4.6 conditional.6
  442.2 5.5 conditional.7
  454.9 4.6 conditional.6
  459.5 5.5 conditional.7
  468.6 3.7 collective-permute-start.1
  474.8 4.6 conditional.6
  479.4 5.5 conditional.7
  488.4 3.7 collective-permute-start.1
  496.6 11.6 collective-permute-start
  508.2 3.7 collective-permute-start.1
  518.4 13.4 %collective-permute-start.1 = (bf16[2,8,8,512]{3,2,1,0:T(8,128)(2,1)}, bf16[2,8,8,512]{3,2,1,0:T(8,128)(2,1)S(1)}, u32[]{:S(2)}, u32[]{:S(2)}) collective-permute-start(bf16[2,8,8,512]{3,2,1,0:T(8,128)(2,1)} %get-tuple-element.1101), channel_id=1, source_target_pairs={{0,8},{8,16},{16,24},{1,9},{9,17},{17,25},{2,10},{10,18},{18,26},{... | collective-permute-start | bytes 393224 | tf_op jit(solution)/shard_map/while/body/eval_jaxpr/ppermute | solution.py:16
  537.2 4.8 broadcast_in_dim.52
  542.1 243.6 %while.46 = (s32[]{:T(128)}, bf16[2,8,8,512]{3,2,1,0:T(8,128)(2,1)}, f32[4608,512]{1,0:T(8,128)}, f32[512,256]{1,0:T(8,128)S(1)}, f32[256,512]{1,0:T(8,128)S(1)}...) while((s32[]{:T(128)}, ...), condition=%wide.region_18.19_spmd, body=%wide.region_9.18_spmd.sunk | while | flops 1835120128 | bytes 79848096 | solution.py:142
  549.0 4.0 collective-permute-done.2
  556.5 6.9 collective-permute-done.2
  566.8 83.4 %collective-permute-done.2 = bf16[2,8,8,512]{3,2,1,0:T(8,128)(2,1)S(1)} collective-permute-done((bf16[2,8,8,512]{3,2,1,0:T(8,128)(2,1)}, bf16[2,8,8,512]{3,2,1,0:T(8,128)(2,1)S(1)}, u32[]{:S(2)}, u32[]{:S(2)}) %collective-permute-start.2) | collective-permute-done | bytes 131104 | tf_op jit(solution)/shard_map/while/body/eval_jaxpr/ppermute | solution.py:16
  650.2 27.4 %conditional.8 = (bf16[2,8,8,512]{3,2,1,0:T(8,128)(2,1)}, f32[4608,512]{1,0:T(8,128)}, f32[512,256]{1,0:T(8,128)S(1)}, f32[256,512]{1,0:T(8,128)S(1)}) conditional(s32[]{:T(128)} %convert_element_type.233, (f32[4608,512]{1,0:T(8,128)}, f32[512,256]{1,0:T(8,128)S(1)}, f32[256,512]{1,0:T(8,128)S(1)}) %tuple.148, (pred[]{:T(512)}, ...), branch_computations={%region_10.10_spmd, %region_11.0_spmd} | conditional | flops 1834989056 | bytes 78667904 | solution.py:136
  657.5 7.2 convert_reduce_fusion
  664.6 12.4 add.153
  681.2 4.4 collective-permute-done.2
  685.7 27.4 %conditional.8 = (bf16[2,8,8,512]{3,2,1,0:T(8,128)(2,1)}, f32[4608,512]{1,0:T(8,128)}, f32[512,256]{1,0:T(8,128)S(1)}, f32[256,512]{1,0:T(8,128)S(1)}) conditional(s32[]{:T(128)} %convert_element_type.233, (f32[4608,512]{1,0:T(8,128)}, f32[512,256]{1,0:T(8,128)S(1)}, f32[256,512]{1,0:T(8,128)S(1)}) %tuple.148, (pred[]{:T(512)}, ...), branch_computations={%region_10.10_spmd, %region_11.0_spmd} | conditional | flops 1834989056 | bytes 78667904 | solution.py:136
  693.0 7.2 convert_reduce_fusion
  700.1 12.4 add.153
  716.7 4.4 collective-permute-done.2
  721.2 27.4 %conditional.8 = (bf16[2,8,8,512]{3,2,1,0:T(8,128)(2,1)}, f32[4608,512]{1,0:T(8,128)}, f32[512,256]{1,0:T(8,128)S(1)}, f32[256,512]{1,0:T(8,128)S(1)}) conditional(s32[]{:T(128)} %convert_element_type.233, (f32[4608,512]{1,0:T(8,128)}, f32[512,256]{1,0:T(8,128)S(1)}, f32[256,512]{1,0:T(8,128)S(1)}) %tuple.148, (pred[]{:T(512)}, ...), branch_computations={%region_10.10_spmd, %region_11.0_spmd} | conditional | flops 1834989056 | bytes 78667904 | solution.py:136
  728.5 7.2 convert_reduce_fusion
  735.6 12.4 add.153
  752.3 4.4 collective-permute-done.2
  756.7 27.4 %conditional.8 = (bf16[2,8,8,512]{3,2,1,0:T(8,128)(2,1)}, f32[4608,512]{1,0:T(8,128)}, f32[512,256]{1,0:T(8,128)S(1)}, f32[256,512]{1,0:T(8,128)S(1)}) conditional(s32[]{:T(128)} %convert_element_type.233, (f32[4608,512]{1,0:T(8,128)}, f32[512,256]{1,0:T(8,128)S(1)}, f32[256,512]{1,0:T(8,128)S(1)}) %tuple.148, (pred[]{:T(512)}, ...), branch_computations={%region_10.10_spmd, %region_11.0_spmd} | conditional | flops 1834989056 | bytes 78667904 | solution.py:136
  764.0 7.2 convert_reduce_fusion
  771.1 12.4 add.153
  786.9 4.3 convert_bitcast_fusion
  791.2 34.9 %copy.11 = bf16[1,1,4608,512]{3,1,2,0:T(2,128)(2,1)S(1)} copy(bf16[1,1,4608,512]{3,2,1,0:T(8,128)(2,1)S(1)} %convert_bitcast_fusion) | data formatting | bytes 9437184
  826.2 98.7 %pad_maximum_fusion = bf16[1,2621440]{1,0:T(2,128)(2,1)} fusion(bf16[1,131072]{1,0:T(2,128)(2,1)S(1)} %bitcast.169, bf16[1,131072]{1,0:T(2,128)(2,1)S(1)} %bitcast.170, bf16[1,2359296]{1,0:T(2,128)(2,1)S(1)} %bitcast.166), kind=kLoop, calls=%fused_computation.165 | loop fusion | flops 15728640 | bytes 10485760 | tf_op jit(solution)/shard_map/concatenate | solution.py:149
  926.8 322.9 %all-reduce.15.cloned.1.call-done = bf16[1,2621440]{1,0:T(2,128)(2,1)} async-done(((bf16[1,2621440]{1,0:T(2,128)(2,1)}), bf16[1,2621440]{1,0:T(2,128)(2,1)}) %all-reduce.15.cloned.1.call-update) | async-done | bytes 5242896
  1249.7 6.0 multiply_add_fusion
  (370 shorter events, 156.9 us)
Async XLA Ops:
  7.2 157.3 %all-gather.3.cloned.1.call-start = ((), (), s32[]{:S(2)}) async-start(), calls=%async_computation | async-start | bytes 11796480 | tf_op jit(solution)/shard_map/all_gather | solution.py:67
  10.8 1.3 copy-start.1
  10.8 305.5 %all-gather.5.cloned.1.call-start = ((), (), s32[]{:S(2)}) async-start(), calls=%async_computation.1 | async-start | bytes 11796480 | tf_op jit(solution)/shard_map/all_gather | solution.py:68
  14.2 1235.5 %all-reduce.15.cloned.1.call-start = ((), (), s32[]{:S(2)}) async-start(), calls=%async_computation.2 | async-start | bytes 20971520
  411.2 1.7 copy-start.6
  413.0 6.2 collective-permute-start
  414.3 11.1 collective-permute-start.1
  432.5 3.4 collective-permute-start
  433.8 8.3 collective-permute-start.1
  449.3 4.1 collective-permute-start
  450.6 9.0 collective-permute-start.1
  466.7 6.5 collective-permute-start
  468.6 10.8 collective-permute-start.1
  486.5 6.5 collective-permute-start
  488.4 6.8 collective-permute-start.1
  496.6 16.1 %collective-permute-start = (bf16[2,8,8,512]{3,2,1,0:T(8,128)(2,1)}, bf16[2,8,8,512]{3,2,1,0:T(8,128)(2,1)S(1)}, u32[]{:S(2)}, u32[]{:S(2)}) collective-permute-start(bf16[2,8,8,512]{3,2,1,0:T(8,128)(2,1)} %get-tuple-element.1100), channel_id=1, source_target_pairs={{0,8},{8,16},{16,24},{1,9},{9,17},{17,25},{2,10},{10,18},{18,26},{... | collective-permute-start | bytes 393224 | tf_op jit(solution)/shard_map/while/body/eval_jaxpr/ppermute | solution.py:16
  508.2 6.9 collective-permute-start.1
  516.4 16.2 %collective-permute-start = (bf16[2,8,8,512]{3,2,1,0:T(8,128)(2,1)}, bf16[2,8,8,512]{3,2,1,0:T(8,128)(2,1)S(1)}, u32[]{:S(2)}, u32[]{:S(2)}) collective-permute-start(bf16[2,8,8,512]{3,2,1,0:T(8,128)(2,1)} %get-tuple-element.1100), channel_id=1, source_target_pairs={{0,8},{8,16},{16,24},{1,9},{9,17},{17,25},{2,10},{10,18},{18,26},{... | collective-permute-start | bytes 393224 | tf_op jit(solution)/shard_map/while/body/eval_jaxpr/ppermute | solution.py:16
  518.4 16.5 %collective-permute-start.1 = (bf16[2,8,8,512]{3,2,1,0:T(8,128)(2,1)}, bf16[2,8,8,512]{3,2,1,0:T(8,128)(2,1)S(1)}, u32[]{:S(2)}, u32[]{:S(2)}) collective-permute-start(bf16[2,8,8,512]{3,2,1,0:T(8,128)(2,1)} %get-tuple-element.1101), channel_id=1, source_target_pairs={{0,8},{8,16},{16,24},{1,9},{9,17},{17,25},{2,10},{10,18},{18,26},{... | collective-permute-start | bytes 393224 | tf_op jit(solution)/shard_map/while/body/eval_jaxpr/ppermute | solution.py:16
  536.4 5.6 copy-start.3
  542.2 3.5 collective-permute-start.2
  547.0 6.1 collective-permute-start.2
  554.4 9.0 collective-permute-start.2
  564.7 85.4 %collective-permute-start.2 = (bf16[2,8,8,512]{3,2,1,0:T(8,128)(2,1)}, bf16[2,8,8,512]{3,2,1,0:T(8,128)(2,1)S(1)}, u32[]{:S(2)}, u32[]{:S(2)}) collective-permute-start(bf16[2,8,8,512]{3,2,1,0:T(8,128)(2,1)} %get-tuple-element.1162), channel_id=1, source_target_pairs={{8,0},{16,8},{24,16},{9,1},{17,9},{25,17},{10,2},{18,10},{26,18},{... | collective-permute-start | bytes 393224 | tf_op jit(solution)/shard_map/while/body/eval_jaxpr/ppermute | solution.py:16
  650.4 4.2 slice-start
  650.5 4.1 slice-start.1
  679.2 6.5 collective-permute-start.2
  686.0 4.2 slice-start
  686.0 4.1 slice-start.1
  714.7 6.5 collective-permute-start.2
  721.5 4.2 slice-start
  721.5 4.1 slice-start.1
  750.2 6.5 collective-permute-start.2
  757.0 4.2 slice-start
  757.0 4.1 slice-start.1
  785.7 0.8 copy-start.4
  924.9 0.7 copy-start.5
  924.9 324.8 %copy-start = (f32[1,327680]{1,0:T(1,128)S(1)}, f32[1,327680]{1,0:T(1,128)}, u32[]{:S(2)}) copy-start(f32[1,327680]{1,0:T(1,128)} %param.24) | copy-start | bytes 3932164
  924.9 324.8 %copy-start.2 = (f32[1,327680]{1,0:T(1,128)S(1)}, f32[1,327680]{1,0:T(1,128)}, u32[]{:S(2)}) copy-start(f32[1,327680]{1,0:T(1,128)} %param.25) | copy-start | bytes 3932164
Sparse Core Ops, SparseCore 0:
  10.9 153.5 all-gather.2
  167.3 149.0 all-gather.4
  925.0 324.6 all-reduce.14
where the time goes:
time: 1270 us; the launch traced here: 1260 us
  waiting for transfers between devices  639 us (50%)
  local copies, waits for them, and re-layouts  247 us (19%)
  other arithmetic  218 us (17%)
  matrix products  79.3 us (6%)
  starting transfers between devices  62.4 us (5%)
  between operations  15 us (1%)
    unnamed x4, waiting for transfers between devices  323 us
    slice x2, local copies, waits for them, and re-layouts, split_row(): kernel = row[:tap_count].reshape(9 * channels, channels)  164 us
    all_gather x1, waiting for transfers between devices, per_device(): lax.all_gather(student_params.astype(jnp.bfloat16), 'dp', axis=1, tiled=T...  150 us
    ppermute x21, waiting for transfers between devices, from_behind(): return lax.ppermute(array, axis, pairs)  109 us
    concatenate x1, other arithmetic, per_device(): jnp.concatenate([totals[0].reshape(-1), totals[1].reshape(-1), totals[2]....  98.7 us
    dot_general x20, matrix products, gated_block(): jnp.dot(columns.reshape(-1, 9 * channels), kernel, preferred_element_type...  74 us
    ppermute x21, starting transfers between devices, from_behind(): return lax.ppermute(array, axis, pairs)  62.3 us
    all_gather x1, waiting for transfers between devices, per_device(): lax.all_gather(teacher_params.astype(jnp.bfloat16), 'dp', axis=1, tiled=T...  56.7 us
  transfers between devices with their start and end apart: 24, of which 10 were waited for; matrix products, arithmetic and copies ran while one was open for 11% of the time, Pallas kernels for 0%

commit v1 on v0

v1 whole, which is shorter than its diff:
```python
import jax
import jax.numpy as jnp
from jax import lax
from jax.sharding import PartitionSpec as P

SE = 256


ema_keep = 0.99
step_rate = 0.001


def shift(array, axis, by):
    peers = lax.axis_size(axis)
    pairs = [(i, i + by) for i in range(peers) if 0 <= i + by < peers]
    return lax.ppermute(array, axis, pairs)


def split_rows(rows, channels, squeeze):
    taps = 9 * channels
    kernel = rows[:taps]
    pair = channels * squeeze // channels
    reduce_w = rows[taps : taps + pair].reshape(channels, squeeze)
    expand_w = rows[taps + pair :].reshape(squeeze, channels)
    return (kernel, reduce_w, expand_w)


def unfold(images):
    side_h, side_w, channels = images.shape[1:]
    padded = jnp.pad(images, ((0, 0), (1, 1), (1, 1), (0, 0)))
    columns = jnp.concatenate(
        [
            padded[:, row_off : row_off + side_h, col_off : col_off + side_w, :]
            for row_off in range(3)
            for col_off in range(3)
        ],
        axis=-1,
    )
    return columns.reshape(-1, 9 * channels)


def forward(images, kernel, reduce_w, expand_w):
    mixed = jnp.dot(unfold(images), kernel, preferred_element_type=jnp.float32)
    mixed = mixed.reshape(images.shape)
    active = jax.nn.silu(mixed)
    pooled = jnp.mean(active, axis=(1, 2)).astype(jnp.bfloat16)
    squeezed = jnp.dot(pooled, reduce_w, preferred_element_type=jnp.float32)
    hidden = jax.nn.silu(squeezed).astype(jnp.bfloat16)
    gate = jax.nn.sigmoid(jnp.dot(hidden, expand_w, preferred_element_type=jnp.float32))
    out = (images.astype(jnp.float32) + active * gate[:, None, None, :]).astype(jnp.bfloat16)
    return out, (mixed, pooled, squeezed, hidden, gate)


def silu_slope(value):
    sig = jax.nn.sigmoid(value)
    return sig * (1.0 + value * (1.0 - sig))


def pull_back(cotangent, kernel, reduce_w, expand_w, held):
    mixed, pooled, squeezed, hidden, gate = held
    images, side_h, side_w, channels = mixed.shape
    grad = cotangent.astype(jnp.float32)
    d_gate = jnp.sum(grad * jax.nn.silu(mixed), axis=(1, 2)) * gate * (1.0 - gate)
    d_gate = d_gate.astype(jnp.bfloat16)
    d_hidden = lax.dot_general(
        d_gate, expand_w, (((1,), (1,)), ((), ())), preferred_element_type=jnp.float32
    )
    d_squeezed = (d_hidden * silu_slope(squeezed)).astype(jnp.bfloat16)
    d_pooled = lax.dot_general(
        d_squeezed, reduce_w, (((1,), (1,)), ((), ())), preferred_element_type=jnp.float32
    ) / (side_h * side_w)
    d_mixed = (grad * gate[:, None, None, :] + d_pooled[:, None, None, :]) * silu_slope(mixed)
    d_mixed = d_mixed.astype(jnp.bfloat16).reshape(-1, channels)
    d_columns = lax.dot_general(
        d_mixed, kernel, (((1,), (1,)), ((), ())), preferred_element_type=jnp.float32
    ).astype(jnp.bfloat16)
    d_columns = d_columns.reshape(images, side_h, side_w, 9, channels)
    total = grad
    for tap in range(9):
        row, col = tap // 3 - 1, tap % 3 - 1
        piece = d_columns[:, :, :, tap].astype(jnp.float32)
        piece = lax.pad(
            piece,
            jnp.float32(0),
            ((0, 0, 0), (row, -row, 0), (col, -col, 0), (0, 0, 0)),
        )
        total = total + piece
    return total.astype(jnp.bfloat16), (d_mixed, d_gate, d_squeezed)


def transposed_dot(left, right):
    return lax.dot_general(
        left, right, (((0,), (0,)), ((), ())), preferred_element_type=jnp.float32
    ).astype(jnp.bfloat16)


def per_device(student_in, teacher_in, out_grad, student_params, teacher_params):
    shape = student_in.shape
    channels = shape[-1]
    flat = (shape[0] * shape[1],) + shape[2:]
    sections = lax.axis_size("segment")
    section = lax.axis_index("segment")
    student_own = student_params.reshape(-1, channels)
    teacher_own = teacher_params.reshape(-1, channels)
    student_rows = lax.all_gather(student_own.astype(jnp.bfloat16), "dp", axis=0, tiled=True)
    student_rows, teacher_own = lax.optimization_barrier((student_rows, teacher_own))
    teacher_rows = lax.all_gather(teacher_own.astype(jnp.bfloat16), "dp", axis=0, tiled=True)
    student_w = split_rows(student_rows, channels, SE)

    current = student_in.reshape(flat)
    for step in range(sections):
        result, held = forward(current, *student_w)
        if step + 1 < sections:
            got = shift(result, "segment", 1)
            current = jnp.where(section == step + 1, got, current)

    grad = out_grad.reshape(flat)
    for step in range(sections):
        result, parts = pull_back(grad, *student_w, held)
        if step + 1 < sections:
            got = shift(result, "segment", -1)
            grad = jnp.where(section == sections - 2 - step, got, grad)
    input_grads = result

    d_mixed, d_gate, d_squeezed = parts
    _, pooled, _, hidden, _ = held
    rows = jnp.concatenate(
        [
            transposed_dot(unfold(current), d_mixed),
            transposed_dot(pooled, d_squeezed).reshape(-1, channels),
            transposed_dot(hidden, d_gate).reshape(-1, channels),
        ],
        axis=0,
    )
    grad_own = lax.psum_scatter(rows, "dp", scatter_dimension=0, tiled=True).astype(jnp.float32)

    teacher_w = split_rows(teacher_rows, channels, SE)
    teacher_now, _ = lax.optimization_barrier((teacher_in.reshape(flat), rows))
    for step in range(sections):
        teacher_out, _ = forward(teacher_now, *teacher_w)
        if step + 1 < sections:
            got = shift(teacher_out, "segment", 1)
            teacher_now = jnp.where(section == step + 1, got, teacher_now)

    grad_shard = grad_own.reshape(student_params.shape)
    teacher_new = ema_keep * teacher_params + (1.0 - ema_keep) * (
        student_params - step_rate * grad_shard
    )
    return (
        teacher_out.reshape((1,) + shape),
        input_grads.reshape((1,) + shape),
        grad_shard,
        teacher_new,
    )


def solution(mesh):
    placed = (
        P(None, "dp", None, None, None),
        P(None, "dp", None, None, None),
        P(None, "dp", None, None, None),
        P("segment", "dp"),
        P("segment", "dp"),
    )
    return jax.shard_map(
        per_device,
        mesh=mesh,
        in_specs=placed,
        out_specs=(
            P("segment", None, "dp", None, None, None),
            P("segment", None, "dp", None, None, None),
            P("segment", "dp"),
            P("segment", "dp"),
        ),
        check_vma=False,
    )
```

time: 1270 us -> 442 us (0.35)
  waiting for transfers between devices: 639 us -> 204 us
  local copies, waits for them, and re-layouts: 247 us -> 33.9 us
  other arithmetic: 218 us -> 58.9 us
  starting transfers between devices: 62.4 us -> 39 us
    unnamed x4 -> x3, waiting for transfers between devices: 323 us -> 0.05 us
    slice x4 -> x3, local copies, waits for them, and re-layouts: 173 us -> 0.97 us  [split_rows(): reduce_w = rows[taps:taps + pair].reshape(channels, squeeze)]
    all_gather x2, waiting for transfers between devices: 207 us -> 119 us  [the longest x1 65.8 us: per_device(): lax.all_gather(student_own.astype(jnp.bfloat16), 'dp', axis=0, tiled=True)]
    concatenate x1, other arithmetic: 98.7 us -> 11.7 us  [per_device(): jnp.concatenate([transposed_dot(unfold(current), d_mixed), transposed_dot...]
    ppermute x21 -> x9, waiting for transfers between devices: 109 us -> 33.1 us  [shift(): return lax.ppermute(array, axis, pairs)]
    reduce_scatter x0 -> x1, waiting for transfers between devices: none -> 51.9 us  [per_device(): lax.psum_scatter(rows, 'dp', scatter_dimension=0, tiled=True)]
    add x12 -> x0, other arithmetic: 50.4 us -> none  [the longest x4 49.4 us: compute(): sums_in[0] + jnp.sum(d_kern.astype(jnp.float32), axis=0)]
    scatter x21 -> x0, other arithmetic: 27.8 us -> none  [the longest x7 11.2 us: student_part(): saved.at[slot_now].set(jnp.where(active_step, picture, saved[slot_now]))]
  transfers between devices with their start and end apart: 24 -> 12, of which waited for: 10 -> 10; matrix products, arithmetic and copies ran while one was open for 11% -> 20% of each run, Pallas kernels for 0% -> 0%
where the time goes in v1:
time: 442 us; the launch traced here: 437 us
  waiting for transfers between devices  204 us (46%)
  matrix products  85.9 us (19%)
  other arithmetic  58.9 us (13%)
  starting transfers between devices  39 us (9%)
  local copies, waits for them, and re-layouts  33.9 us (8%)
  between operations  15.1 us (3%)
    all_gather x1, waiting for transfers between devices, per_device(): lax.all_gather(student_own.astype(jnp.bfloat16), 'dp', axis=0, tiled=True)  65.8 us
    all_gather x1, waiting for transfers between devices, per_device(): lax.all_gather(teacher_own.astype(jnp.bfloat16), 'dp', axis=0, tiled=True)  53.6 us
    reduce_scatter x1, waiting for transfers between devices, per_device(): lax.psum_scatter(rows, 'dp', scatter_dimension=0, tiled=True)  51.9 us
    dot_general x8, matrix products, forward(): mixed = jnp.dot(unfold(images), kernel, preferred_element_type=jnp.float32)  41.2 us
    ppermute x9, starting transfers between devices, shift(): return lax.ppermute(array, axis, pairs)  38.6 us
    ppermute x9, waiting for transfers between devices, shift(): return lax.ppermute(array, axis, pairs)  33.1 us
    unnamed x98, local copies, waits for them, and re-layouts  23.1 us
    dot_general x4, matrix products, pull_back(): lax.dot_general(d_mixed, kernel, (((1,), (1,)), ((), ())), preferred_elem...  22.5 us
  transfers between devices with their start and end apart: 12, of which 10 were waited for; matrix products, arithmetic and copies ran while one was open for 20% of the time, Pallas kernels for 0%

profile of v1, /device:TPU:0, one launch (start us, length us, event | category | flops | bytes accessed | tf_op | source)
XLA Modules:
  0.0 437.1 jit_solution(14040566368446099864)
XLA Ops:
  7.2 14.7 %convert_reduce_fusion = bf16[327680]{0:T(1024)(128)(2,1)S(1)} fusion(f32[1,327680]{1,0:T(1,128)} %param.8), kind=kLoop, calls=%fused_computation.97 | loop fusion | flops 327680 | bytes 1966080 | tf_op jit(solution)/shard_map/convert_element_type | solution.py:105
  24.0 13.0 %reduce.5 = bf16[327680]{0:T(1024)(128)(2,1)S(1)} reduce(f32[1,327680]{1,0:T(1,128)S(1)} %copy-done.2, f32[]{:T(128)} %broadcast.214), dimensions={0}, to_apply=%param.9.reduce_sub_computation.3 | reduce | bytes 1966084 | tf_op args[4]
  46.5 65.8 %all-gather.3.cloned.1.call-done = bf16[5120,512]{1,0:T(8,128)(2,1)} async-done(((bf16[640,512]{1,0:T(8,128)(2,1)}), bf16[5120,512]{1,0:T(8,128)(2,1)}) %all-gather.3.cloned.1.call-update) | async-done | bytes 5242896 | tf_op jit(solution)/shard_map/all_gather | solution.py:105
  112.3 6.1 %fusion.251 = (f32[8,512]{1,0:T(8,128)S(1)}, f32[8,8,8,512]{3,2,1,0:T(8,128)S(1)}) fusion(bf16[8,8,8,4608]{3,2,1,0:T(8,128)(2,1)} %fusion.114, bf16[5120,512]{1,0:T(8,128)(2,1)} %all-gather.3.cloned.1.call-done), kind=kOutput, calls=%fused_computation.449 | convolution fusion | flops 2417225728 | bytes 10502144 | tf_op jit(solution)/shard_map/dot_general | solution.py:43
  118.5 1.3 fusion.35
  120.0 1.3 collective-permute-start
  121.4 1.5 collective-permute-done
  123.8 1.6 copy-done.8
  125.4 2.8 fusion.252
  129.7 8.9 %collective-permute-start.1 = (bf16[8,8,8,512]{3,2,1,0:T(8,128)(2,1)S(1)}, bf16[8,8,8,512]{3,2,1,0:T(8,128)(2,1)S(1)}, u32[]{:S(2)}, u32[]{:S(2)}) collective-permute-start(bf16[8,8,8,512]{3,2,1,0:T(8,128)(2,1)S(1)} %add_convert_fusion.5), channel_id=1, source_target_pairs={{0,8},{8,16},{16,24},{1,9},{9,17},{17,25},{2,10},{10,18},{18,26},{... | collective-permute-start | bytes 1572872 | tf_op jit(solution)/shard_map/ppermute | solution.py:16
  140.8 6.3 %fusion.253 = (f32[8,512]{1,0:T(8,128)S(1)}, f32[8,8,8,512]{3,2,1,0:T(8,128)S(1)}) fusion(bf16[8,8,8,4608]{3,2,1,0:T(8,128)(2,1)S(1)} %fusion.130, bf16[5120,512]{1,0:T(8,128)(2,1)} %all-gather.3.cloned.1.call-done), kind=kOutput, calls=%fused_computation.451 | convolution fusion | flops 2417225728 | bytes 10502144 | tf_op jit(solution)/shard_map/dot_general | solution.py:43
  148.7 9.0 %collective-permute-start.2 = (bf16[8,8,8,512]{3,2,1,0:T(8,128)(2,1)S(1)}, bf16[8,8,8,512]{3,2,1,0:T(8,128)(2,1)S(1)}, u32[]{:S(2)}, u32[]{:S(2)}) collective-permute-start(bf16[8,8,8,512]{3,2,1,0:T(8,128)(2,1)S(1)} %add_convert_fusion.4), channel_id=1, source_target_pairs={{0,8},{8,16},{16,24},{1,9},{9,17},{17,25},{2,10},{10,18},{18,26},{... | collective-permute-start | bytes 1572872 | tf_op jit(solution)/shard_map/ppermute | solution.py:16
  157.7 1.5 collective-permute-done.2
  160.3 7.2 %fusion.250 = (f32[8,512]{1,0:T(8,128)S(1)}, f32[8,512]{1,0:T(8,128)S(1)}, f32[8,8,8,512]{3,2,1,0:T(8,128)S(1)}) fusion(bf16[4,2,8,8,512]{4,3,2,1,0:T(8,128)(2,1)S(1)} %copy-done.5, bf16[8,8,8,4608]{3,2,1,0:T(8,128)(2,1)S(1)} %fusion.138, bf16[5120,512]{1,0:T(8,128)(2,1)} %all-gather.3.cloned.1.call-done), kind=kOutput, calls=%fused_computation.448 | convolution fusion | flops 2418008064 | bytes 11042816 | tf_op jit(solution)/shard_map/dot_general | solution.py:43
  167.8 1.3 convolution_multiply_fusion.3
  169.7 5.2 %convolution_convert_fusion.3 = bf16[512,4608]{1,0:T(8,128)(2,1)S(1)} fusion(bf16[512,512]{1,0:T(8,128)(2,1)S(1)} %bitcast.297, bf16[5120,512]{1,0:T(8,128)(2,1)} %all-gather.3.cloned.1.call-done), kind=kOutput, calls=%fused_computation.4 | convolution fusion | flops 2418278400 | bytes 9961472 | tf_op jit(solution)/shard_map/dot_general | solution.py:74
  176.6 1.7 collective-permute-start.3
  178.3 8.7 %collective-permute-done.3 = bf16[8,8,8,512]{3,2,1,0:T(8,128)(2,1)S(1)} collective-permute-done((bf16[8,8,8,512]{3,2,1,0:T(8,128)(2,1)S(1)}, bf16[8,8,8,512]{3,2,1,0:T(8,128)(2,1)S(1)}, u32[]{:S(2)}, u32[]{:S(2)}) %collective-permute-start.3) | collective-permute-done | bytes 524320 | tf_op jit(solution)/shard_map/ppermute | solution.py:16
  187.4 1.3 convolution_multiply_fusion.2
  189.2 5.2 %convolution_convert_fusion.2 = bf16[512,4608]{1,0:T(8,128)(2,1)S(1)} fusion(bf16[512,512]{1,0:T(8,128)(2,1)S(1)} %bitcast.298, bf16[5120,512]{1,0:T(8,128)(2,1)} %all-gather.3.cloned.1.call-done), kind=kOutput, calls=%fused_computation.3 | convolution fusion | flops 2418278400 | bytes 9961472 | tf_op jit(solution)/shard_map/dot_general | solution.py:74
  196.1 1.3 collective-permute-start.4
  197.4 9.9 %collective-permute-done.4 = bf16[8,8,8,512]{3,2,1,0:T(8,128)(2,1)S(1)} collective-permute-done((bf16[8,8,8,512]{3,2,1,0:T(8,128)(2,1)S(1)}, bf16[8,8,8,512]{3,2,1,0:T(8,128)(2,1)S(1)}, u32[]{:S(2)}, u32[]{:S(2)}) %collective-permute-start.4) | collective-permute-done | bytes 524320 | tf_op jit(solution)/shard_map/ppermute | solution.py:16
  207.7 1.3 convolution_multiply_fusion.1
  209.6 5.2 %convolution_convert_fusion.1 = bf16[512,4608]{1,0:T(8,128)(2,1)S(1)} fusion(bf16[512,512]{1,0:T(8,128)(2,1)S(1)} %bitcast.299, bf16[5120,512]{1,0:T(8,128)(2,1)} %all-gather.3.cloned.1.call-done), kind=kOutput, calls=%fused_computation.2 | convolution fusion | flops 2418278400 | bytes 9961472 | tf_op jit(solution)/shard_map/dot_general | solution.py:74
  216.4 1.3 collective-permute-start.5
  218.0 9.0 %collective-permute-done.5 = bf16[8,8,8,512]{3,2,1,0:T(8,128)(2,1)S(1)} collective-permute-done((bf16[8,8,8,512]{3,2,1,0:T(8,128)(2,1)S(1)}, bf16[8,8,8,512]{3,2,1,0:T(8,128)(2,1)S(1)}, u32[]{:S(2)}, u32[]{:S(2)}) %collective-permute-start.5) | collective-permute-done | bytes 524320 | tf_op jit(solution)/shard_map/ppermute | solution.py:16
  227.3 1.3 fusion.39
  229.9 6.7 %bitcast_convert_fusion = bf16[4608,512]{1,0:T(8,128)(2,1)S(1)} fusion(bf16[8,8,8,4608]{3,2,1,0:T(8,128)(2,1)} %copy-done.9, bf16[8,8,8,512]{3,2,1,0:T(8,128)(2,1)S(1)} %fusion.81), kind=kOutput, calls=%fused_computation | convolution fusion | flops 2418278400 | bytes 9961472 | tf_op jit(solution)/shard_map/dot_general | solution.py:92
  236.6 11.7 %pad_maximum_fusion = bf16[5120,512]{1,0:T(8,128)(2,1)} fusion(bf16[256,512]{1,0:T(8,128)(2,1)S(1)} %convolution_convert_fusion.4, bf16[256,512]{1,0:T(8,128)(2,1)S(1)} %reshape.234, bf16[4608,512]{1,0:T(8,128)(2,1)S(1)} %bitcast_convert_fusion), kind=kLoop, calls=%fused_computation.5 | loop fusion | flops 15728640 | bytes 10485760 | tf_op jit(solution)/shard_map/concatenate | solution.py:127
  256.7 53.6 %all-gather.5.cloned.1.call-done = bf16[5120,512]{1,0:T(8,128)(2,1)} async-done(((bf16[640,512]{1,0:T(8,128)(2,1)}), bf16[5120,512]{1,0:T(8,128)(2,1)}) %all-gather.5.cloned.1.call-update) | async-done | bytes 5242896 | tf_op jit(solution)/shard_map/all_gather | solution.py:107
  311.4 6.0 %fusion.254 = (f32[8,512]{1,0:T(8,128)S(1)}, f32[8,8,8,512]{3,2,1,0:T(8,128)S(1)}) fusion(bf16[8,8,8,4608]{3,2,1,0:T(8,128)(2,1)} %fusion.146, bf16[5120,512]{1,0:T(8,128)(2,1)} %all-gather.5.cloned.1.call-done), kind=kOutput, calls=%fused_computation.452 | convolution fusion | flops 2417225728 | bytes 10502144 | tf_op jit(solution)/shard_map/dot_general | solution.py:43
  317.4 1.3 fusion.23
  318.9 1.5 collective-permute-start.6
  322.7 6.3 %fusion.255 = (f32[8,512]{1,0:T(8,128)S(1)}, f32[8,8,8,512]{3,2,1,0:T(8,128)S(1)}) fusion(bf16[8,8,8,4608]{3,2,1,0:T(8,128)(2,1)S(1)} %fusion.154, bf16[5120,512]{1,0:T(8,128)(2,1)} %all-gather.5.cloned.1.call-done), kind=kOutput, calls=%fused_computation.453 | convolution fusion | flops 2417225728 | bytes 10502144 | tf_op jit(solution)/shard_map/dot_general | solution.py:43
  329.0 1.3 fusion.20
  330.5 8.7 %collective-permute-start.7 = (bf16[8,8,8,512]{3,2,1,0:T(8,128)(2,1)S(1)}, bf16[8,8,8,512]{3,2,1,0:T(8,128)(2,1)S(1)}, u32[]{:S(2)}, u32[]{:S(2)}) collective-permute-start(bf16[8,8,8,512]{3,2,1,0:T(8,128)(2,1)S(1)} %add_convert_fusion.2), channel_id=1, source_target_pairs={{0,8},{8,16},{16,24},{1,9},{9,17},{17,25},{2,10},{10,18},{18,26},{... | collective-permute-start | bytes 1572872 | tf_op jit(solution)/shard_map/ppermute | solution.py:16
  339.3 6.8 %convolution_convert_fusion = bf16[512,4608]{1,0:T(8,128)(2,1)} fusion(bf16[512,512]{1,0:T(8,128)(2,1)S(1)} %bitcast.295, bf16[5120,512]{1,0:T(8,128)(2,1)} %all-gather.3.cloned.1.call-done), kind=kOutput, calls=%fused_computation.1 | convolution fusion | flops 2418278400 | bytes 9961472 | tf_op jit(solution)/shard_map/dot_general | solution.py:74
  347.0 2.8 fusion.256
  349.8 1.3 fusion.17
  351.3 4.8 %collective-permute-start.8 = (bf16[8,8,8,512]{3,2,1,0:T(8,128)(2,1)S(1)}, bf16[8,8,8,512]{3,2,1,0:T(8,128)(2,1)S(1)}, u32[]{:S(2)}, u32[]{:S(2)}) collective-permute-start(bf16[8,8,8,512]{3,2,1,0:T(8,128)(2,1)S(1)} %add_convert_fusion.1), channel_id=1, source_target_pairs={{0,8},{8,16},{16,24},{1,9},{9,17},{17,25},{2,10},{10,18},{18,26},{... | collective-permute-start | bytes 1572872 | tf_op jit(solution)/shard_map/ppermute | solution.py:16
  356.1 2.7 slice_bitcast_fusion.13
  358.8 3.0 fusion.91
  363.1 3.7 fusion.257
  366.8 1.4 fusion.14
  368.2 2.2 add_convert_fusion
  370.4 51.9 %reduce-scatter.2.cloned.1.call-done = bf16[640,512]{1,0:T(8,128)(2,1)} async-done(((bf16[5120,512]{1,0:T(8,128)(2,1)}), bf16[640,512]{1,0:T(8,128)(2,1)}) %reduce-scatter.2.cloned.1.call-update) | async-done | bytes 655376 | tf_op jit(solution)/shard_map/reduce_scatter | solution.py:135
  423.5 1.3 copy.84
  424.9 5.4 %multiply_add_fusion = f32[1,327680]{1,0:T(1,128)} fusion(f32[1,327680]{1,0:T(1,128)} %param.8, f32[1,327680]{1,0:T(1,128)S(1)} %bitcast.283, f32[1,327680]{1,0:T(1,128)S(1)} %copy-done.3), kind=kLoop, calls=%fused_computation.96 | loop fusion | flops 1638400 | bytes 5242880 | tf_op jit(solution)/shard_map/add | solution.py:146
  (159 shorter events, 43.9 us)
Async XLA Ops:
  7.2 16.8 %copy-start.2 = (f32[1,327680]{1,0:T(1,128)S(1)}, f32[1,327680]{1,0:T(1,128)}, u32[]{:S(2)}) copy-start(f32[1,327680]{1,0:T(1,128)} %param.9) | copy-start | bytes 3932164
  7.2 31.0 %copy-start = (bf16[4,2,8,8,512]{4,3,2,1,0:T(8,128)(2,1)S(1)}, bf16[4,2,8,8,512]{4,3,2,1,0:T(8,128)(2,1)}, u32[]{:S(2)}) copy-start(bf16[4,2,8,8,512]{4,3,2,1,0:T(8,128)(2,1)} %param.5) | copy-start | bytes 1572868
  7.2 105.1 %all-gather.3.cloned.1.call-start = ((), (), s32[]{:S(2)}) async-start(), calls=%async_computation.1 | async-start | bytes 5898240 | tf_op jit(solution)/shard_map/all_gather | solution.py:105
  23.2 287.1 %all-gather.5.cloned.1.call-start = ((), (), s32[]{:S(2)}) async-start(), calls=%async_computation.2 | async-start | bytes 5898240 | tf_op jit(solution)/shard_map/all_gather | solution.py:107
  112.3 6.1 %slice-start.2 = ((bf16[5120,512]{1,0:T(8,128)(2,1)}), bf16[256,512]{1,0:T(8,128)(2,1)S(1)}, s32[]{:S(2)}) async-start(bf16[5120,512]{1,0:T(8,128)(2,1)} %all-gather.3.cloned.1.call-done), calls=%async_computation.6 | async-start | bytes 524288 | tf_op jit(solution)/shard_map/slice | solution.py:23
  120.0 2.8 collective-permute-start
  122.9 2.5 copy-start.8
  129.7 10.2 %collective-permute-start.1 = (bf16[8,8,8,512]{3,2,1,0:T(8,128)(2,1)S(1)}, bf16[8,8,8,512]{3,2,1,0:T(8,128)(2,1)S(1)}, u32[]{:S(2)}, u32[]{:S(2)}) collective-permute-start(bf16[8,8,8,512]{3,2,1,0:T(8,128)(2,1)S(1)} %add_convert_fusion.5), channel_id=1, source_target_pairs={{0,8},{8,16},{16,24},{1,9},{9,17},{17,25},{2,10},{10,18},{18,26},{... | collective-permute-start | bytes 1572872 | tf_op jit(solution)/shard_map/ppermute | solution.py:16
  148.7 10.5 %collective-permute-start.2 = (bf16[8,8,8,512]{3,2,1,0:T(8,128)(2,1)S(1)}, bf16[8,8,8,512]{3,2,1,0:T(8,128)(2,1)S(1)}, u32[]{:S(2)}, u32[]{:S(2)}) collective-permute-start(bf16[8,8,8,512]{3,2,1,0:T(8,128)(2,1)S(1)} %add_convert_fusion.4), channel_id=1, source_target_pairs={{0,8},{8,16},{16,24},{1,9},{9,17},{17,25},{2,10},{10,18},{18,26},{... | collective-permute-start | bytes 1572872 | tf_op jit(solution)/shard_map/ppermute | solution.py:16
  159.2 1.0 copy-start.5
  160.0 7.7 %slice-start = ((s8[5242880]{0:T(1024)(128)(4,1)}), s8[4194304]{0:T(1024)(128)(4,1)S(1)}, s32[]{:S(2)}) async-start(s8[5242880]{0:T(1024)(128)(4,1)} %bitcast.293), calls=%async_computation.4 | async-start | bytes 8388608
  160.3 7.2 %copy-start.9 = (bf16[8,8,8,4608]{3,2,1,0:T(8,128)(2,1)}, bf16[8,8,8,4608]{3,2,1,0:T(8,128)(2,1)S(1)}, u32[]{:S(2)}) copy-start(bf16[8,8,8,4608]{3,2,1,0:T(8,128)(2,1)S(1)} %fusion.138) | copy-start | bytes 14155780
  160.3 7.4 %slice-start.1 = ((s8[5242880]{0:T(1024)(128)(4,1)}), s8[1048576]{0:T(1024)(128)(4,1)S(1)}, s32[]{:S(2)}) async-start(s8[5242880]{0:T(1024)(128)(4,1)} %bitcast.293), calls=%async_computation.5 | async-start | bytes 2097152
  176.6 10.4 %collective-permute-start.3 = (bf16[8,8,8,512]{3,2,1,0:T(8,128)(2,1)S(1)}, bf16[8,8,8,512]{3,2,1,0:T(8,128)(2,1)S(1)}, u32[]{:S(2)}, u32[]{:S(2)}) collective-permute-start(bf16[8,8,8,512]{3,2,1,0:T(8,128)(2,1)S(1)} %fusion.52), channel_id=1, source_target_pairs={{8,0},{16,8},{24,16},{9,1},{17,9},{25,17},{10,2},{18,10},{26,18},{... | collective-permute-start | bytes 1572872 | tf_op jit(solution)/shard_map/ppermute | solution.py:16
  196.1 11.2 %collective-permute-start.4 = (bf16[8,8,8,512]{3,2,1,0:T(8,128)(2,1)S(1)}, bf16[8,8,8,512]{3,2,1,0:T(8,128)(2,1)S(1)}, u32[]{:S(2)}, u32[]{:S(2)}) collective-permute-start(bf16[8,8,8,512]{3,2,1,0:T(8,128)(2,1)S(1)} %fusion.65), channel_id=1, source_target_pairs={{8,0},{16,8},{24,16},{9,1},{17,9},{25,17},{10,2},{18,10},{26,18},{... | collective-permute-start | bytes 1572872 | tf_op jit(solution)/shard_map/ppermute | solution.py:16
  216.4 10.5 %collective-permute-start.5 = (bf16[8,8,8,512]{3,2,1,0:T(8,128)(2,1)S(1)}, bf16[8,8,8,512]{3,2,1,0:T(8,128)(2,1)S(1)}, u32[]{:S(2)}, u32[]{:S(2)}) collective-permute-start(bf16[8,8,8,512]{3,2,1,0:T(8,128)(2,1)S(1)} %fusion.78), channel_id=1, source_target_pairs={{8,0},{16,8},{24,16},{9,1},{17,9},{25,17},{10,2},{18,10},{26,18},{... | collective-permute-start | bytes 1572872 | tf_op jit(solution)/shard_map/ppermute | solution.py:16
  217.7 204.6 %reduce-scatter.2.cloned.1.call-start = ((), (), s32[]{:S(2)}) async-start(), calls=%async_computation.3 | async-start | bytes 5898240 | tf_op jit(solution)/shard_map/reduce_scatter | solution.py:135
  227.3 9.3 %copy-start.6 = (bf16[8,8,8,512]{3,2,1,0:T(8,128)(2,1)}, bf16[8,8,8,512]{3,2,1,0:T(8,128)(2,1)S(1)}, u32[]{:S(2)}) copy-start(bf16[8,8,8,512]{3,2,1,0:T(8,128)(2,1)S(1)} %get-tuple-element.13) | copy-start | bytes 1572868
  236.6 11.7 %copy-start.1 = (bf16[4,2,8,8,512]{4,3,2,1,0:T(8,128)(2,1)S(1)}, bf16[4,2,8,8,512]{4,3,2,1,0:T(8,128)(2,1)}, u32[]{:S(2)}) copy-start(bf16[4,2,8,8,512]{4,3,2,1,0:T(8,128)(2,1)} %param.6) | copy-start | bytes 1572868
  318.9 2.8 collective-permute-start.6
  330.5 15.6 %collective-permute-start.7 = (bf16[8,8,8,512]{3,2,1,0:T(8,128)(2,1)S(1)}, bf16[8,8,8,512]{3,2,1,0:T(8,128)(2,1)S(1)}, u32[]{:S(2)}, u32[]{:S(2)}) collective-permute-start(bf16[8,8,8,512]{3,2,1,0:T(8,128)(2,1)S(1)} %add_convert_fusion.2), channel_id=1, source_target_pairs={{0,8},{8,16},{16,24},{1,9},{9,17},{17,25},{2,10},{10,18},{18,26},{... | collective-permute-start | bytes 1572872 | tf_op jit(solution)/shard_map/ppermute | solution.py:16
  339.2 7.8 %slice-start.3 = ((s8[5242880]{0:T(1024)(128)(4,1)}), s8[4194304]{0:T(1024)(128)(4,1)S(1)}, s32[]{:S(2)}) async-start(s8[5242880]{0:T(1024)(128)(4,1)} %bitcast.301), calls=%async_computation.7 | async-start | bytes 8388608
  339.2 7.8 %slice-start.4 = ((s8[5242880]{0:T(1024)(128)(4,1)}), s8[1048576]{0:T(1024)(128)(4,1)S(1)}, s32[]{:S(2)}) async-start(s8[5242880]{0:T(1024)(128)(4,1)} %bitcast.301), calls=%async_computation.8 | async-start | bytes 2097152
  351.3 7.5 %copy-start.7 = (bf16[8,8,8,512]{3,2,1,0:T(8,128)(2,1)S(1)}, bf16[8,8,8,512]{3,2,1,0:T(8,128)(2,1)}, u32[]{:S(2)}) copy-start(bf16[8,8,8,512]{3,2,1,0:T(8,128)(2,1)} %copy-done.6) | copy-start | bytes 1572868
  351.3 10.5 %collective-permute-start.8 = (bf16[8,8,8,512]{3,2,1,0:T(8,128)(2,1)S(1)}, bf16[8,8,8,512]{3,2,1,0:T(8,128)(2,1)S(1)}, u32[]{:S(2)}, u32[]{:S(2)}) collective-permute-start(bf16[8,8,8,512]{3,2,1,0:T(8,128)(2,1)S(1)} %add_convert_fusion.1), channel_id=1, source_target_pairs={{0,8},{8,16},{16,24},{1,9},{9,17},{17,25},{2,10},{10,18},{18,26},{... | collective-permute-start | bytes 1572872 | tf_op jit(solution)/shard_map/ppermute | solution.py:16
  358.8 4.0 slice-start.5
  361.8 1.2 slice-start.6
  366.8 58.1 %copy-start.3 = (f32[1,327680]{1,0:T(1,128)S(1)}, f32[1,327680]{1,0:T(1,128)}, u32[]{:S(2)}) copy-start(f32[1,327680]{1,0:T(1,128)} %param.9) | copy-start | bytes 3932164
  424.9 5.4 %copy-start.4 = (f32[1,1,640,512]{3,1,2,0:T(1,128)}, f32[1,1,640,512]{3,1,2,0:T(1,128)S(1)}, u32[]{:S(2)}) copy-start(f32[1,1,640,512]{3,1,2,0:T(1,128)S(1)} %copy.84) | copy-start | bytes 3932164
Sparse Core Ops, SparseCore 0:
  23.3 88.9 all-gather.2
  217.9 92.3 all-gather.4
  320.6 101.6 reduce-scatter.1

commit v2 on v1

v2 whole, which is shorter than its diff:
```python
import jax
import jax.numpy as jnp
from jax import lax
from jax.experimental import pallas as pl
from jax.experimental.pallas import tpu as pltpu
from jax.sharding import PartitionSpec as P

SE = 256


ema_keep = 0.99
step_rate = 0.001


def hop(array, axis, source, target):
    return lax.ppermute(array, axis, [(source, target)])


def split_rows(rows, channels, squeeze):
    taps = 9 * channels
    reduce_w = rows[taps : taps + squeeze].reshape(channels, squeeze)
    expand_w = rows[taps + squeeze :].reshape(squeeze, channels)
    return (rows, reduce_w, expand_w)


def whole(shape):
    return pl.BlockSpec(shape, lambda *step: (0,) * len(shape))


def params(mega):
    return pltpu.CompilerParams(vmem_limit_bytes=mega * 1024 * 1024)


def to_matrix(flat, channels):
    lanes = 128
    parts = channels // lanes
    rows = flat.shape[1] // channels

    def body(flat_ref, out_ref):
        for part in range(parts):
            piece = flat_ref[pl.ds(part, rows, stride=parts), :]
            out_ref[:, part * lanes : (part + 1) * lanes] = piece.astype(jnp.bfloat16)

    return pl.pallas_call(
        body,
        out_shape=jax.ShapeDtypeStruct((rows, channels), jnp.bfloat16),
        compiler_params=params(24),
        cost_estimate=pl.CostEstimate(
            flops=rows * channels, bytes_accessed=6 * rows * channels, transcendentals=0
        ),
    )(flat.reshape(rows * parts, lanes))


def finish(grad_own, student_params, teacher_params):
    rows, channels = grad_own.shape
    lanes = 128
    parts = channels // lanes

    def body(grad_ref, student_ref, teacher_ref, flat_ref, new_ref):
        for part in range(parts):
            piece = grad_ref[:, part * lanes : (part + 1) * lanes].astype(jnp.float32)
            here = pl.ds(part, rows, stride=parts)
            flat_ref[here, :] = piece
            stepped = student_ref[here, :] - step_rate * piece
            new_ref[here, :] = ema_keep * teacher_ref[here, :] + (1.0 - ema_keep) * stepped

    flat_shape = jax.ShapeDtypeStruct((rows * parts, lanes), jnp.float32)
    flat, new = pl.pallas_call(
        body,
        out_shape=(flat_shape, flat_shape),
        compiler_params=params(24),
        cost_estimate=pl.CostEstimate(
            flops=5 * rows * channels, bytes_accessed=18 * rows * channels, transcendentals=0
        ),
    )(
        grad_own,
        student_params.reshape(rows * parts, lanes),
        teacher_params.reshape(rows * parts, lanes),
    )
    return flat.reshape(student_params.shape), new.reshape(teacher_params.shape)


def spread(values, shifted, side, count):
    line = side * count
    channels = values.shape[-1]
    edge = jnp.zeros((line, channels), jnp.bfloat16)
    grid = values.reshape(side, side, count, channels)
    blank = jnp.zeros((side, 1, count, channels), jnp.float32)
    versions = (
        jnp.concatenate([blank, grid[:, : side - 1]], axis=1),
        grid,
        jnp.concatenate([grid[:, 1:], blank], axis=1),
    )
    for col in range(3):
        shifted[col, :line, :] = edge
        shifted[col, line : line + side * line, :] = (
            versions[col].reshape(side * line, channels).astype(jnp.bfloat16)
        )
        shifted[col, line + side * line :, :] = edge


def silu(value):
    return value / (1.0 + jnp.exp(-value))


def sigmoid(value):
    return 1.0 / (1.0 + jnp.exp(-value))


def silu_slope(value):
    sig = sigmoid(value)
    return sig * (1.0 + value * (1.0 - sig))


def forward(images, rows, reduce_w, expand_w, side, count):
    area, channels = images.shape
    squeeze = reduce_w.shape[1]
    line = side * count

    def body(x_ref, kernel_ref, red_ref, exp_ref, out_ref, mixed_ref, pool_ref, sq_ref, hid_ref, gate_ref, shifted):
        step = pl.program_id(0)

        @pl.when(step == 0)
        def _():
            spread(x_ref[...].astype(jnp.float32), shifted, side, count)
            mixed_ref[...] = jnp.zeros_like(mixed_ref)

        here = pl.ds(pl.multiple_of(step * line, line), area)
        total = mixed_ref[...]
        for col in range(3):
            total += jnp.dot(
                shifted[col, here, :],
                kernel_ref[col * channels : (col + 1) * channels, :],
                preferred_element_type=jnp.float32,
            )
        mixed_ref[...] = total

        @pl.when(step == 2)
        def _():
            active = silu(mixed_ref[...]).reshape(side * side, count, channels)
            pooled = (jnp.sum(active, axis=0) / (side * side)).astype(jnp.bfloat16)
            squeezed = jnp.dot(pooled, red_ref[...], preferred_element_type=jnp.float32)
            hidden = silu(squeezed).astype(jnp.bfloat16)
            gate = sigmoid(jnp.dot(hidden, exp_ref[...], preferred_element_type=jnp.float32))
            x = x_ref[...].astype(jnp.float32).reshape(active.shape)
            out = x + active * gate[None]
            out_ref[...] = out.reshape(area, channels).astype(jnp.bfloat16)
            pool_ref[...] = pooled.astype(jnp.float32)
            sq_ref[...] = squeezed
            hid_ref[...] = hidden.astype(jnp.float32)
            gate_ref[...] = gate

    shapes = (
        ((area, channels), jnp.bfloat16),
        ((area, channels), jnp.float32),
        ((count, channels), jnp.float32),
        ((count, squeeze), jnp.float32),
        ((count, squeeze), jnp.float32),
        ((count, channels), jnp.float32),
    )
    out, *held = pl.pallas_call(
        body,
        grid=(3,),
        in_specs=[
            whole(images.shape),
            pl.BlockSpec((3 * channels, channels), lambda step: (step, 0)),
            whole(reduce_w.shape),
            whole(expand_w.shape),
        ],
        out_specs=[whole(shape) for shape, _ in shapes],
        out_shape=[jax.ShapeDtypeStruct(*shape) for shape in shapes],
        scratch_shapes=[pltpu.VMEM((3, area + 2 * line, channels), jnp.bfloat16)],
        compiler_params=params(40),
        cost_estimate=pl.CostEstimate(
            flops=18 * area * channels * channels, bytes_accessed=8000000, transcendentals=area * channels
        ),
    )(images, rows, reduce_w, expand_w)
    return out, held


def pull_back(cotangent, rows, reduce_w, expand_w, held, side, count):
    mixed, _, squeezed, _, gate = held
    area, channels = cotangent.shape
    squeeze = reduce_w.shape[1]
    line = side * count

    def body(g_ref, mixed_ref, sq_ref, gate_ref, kernel_ref, red_ref, exp_ref, dx_ref, dm_ref, dg_ref, ds_ref, shifted, total_ref):
        step = pl.program_id(0)

        @pl.when(step == 0)
        def _():
            grad = g_ref[...].astype(jnp.float32)
            total_ref[...] = grad
            grad = grad.reshape(side * side, count, channels)
            value = mixed_ref[...].reshape(grad.shape)
            gate_val = gate_ref[...]
            sig = sigmoid(value)
            d_gate = jnp.sum(grad * value * sig, axis=0) * gate_val * (1.0 - gate_val)
            d_hidden = lax.dot_general(
                d_gate.astype(jnp.bfloat16),
                exp_ref[...],
                (((1,), (1,)), ((), ())),
                preferred_element_type=jnp.float32,
            )
            d_squeezed = d_hidden * silu_slope(sq_ref[...])
            d_pooled = lax.dot_general(
                d_squeezed.astype(jnp.bfloat16),
                red_ref[...],
                (((1,), (1,)), ((), ())),
                preferred_element_type=jnp.float32,
            ) / (side * side)
            slope = sig * (1.0 + value * (1.0 - sig))
            d_mixed = (grad * gate_val[None] + d_pooled[None]) * slope
            d_mixed = d_mixed.reshape(area, channels)
            dm_ref[...] = d_mixed.astype(jnp.bfloat16)
            dg_ref[...] = d_gate
            ds_ref[...] = d_squeezed
            spread(d_mixed, shifted, side, count)

        here = pl.ds(pl.multiple_of((2 - step) * line, line), area)
        total = total_ref[...]
        for col in range(3):
            total += lax.dot_general(
                shifted[2 - col, here, :],
                kernel_ref[col * channels : (col + 1) * channels, :],
                (((1,), (1,)), ((), ())),
                preferred_element_type=jnp.float32,
            )
        total_ref[...] = total

        @pl.when(step == 2)
        def _():
            dx_ref[...] = total_ref[...].astype(jnp.bfloat16)

    shapes = (
        ((area, channels), jnp.bfloat16),
        ((area, channels), jnp.bfloat16),
        ((count, channels), jnp.float32),
        ((count, squeeze), jnp.float32),
    )
    d_in, *parts = pl.pallas_call(
        body,
        grid=(3,),
        in_specs=[
            whole(cotangent.shape),
            whole(mixed.shape),
            whole(squeezed.shape),
            whole(gate.shape),
            pl.BlockSpec((3 * channels, channels), lambda step: (step, 0)),
            whole(reduce_w.shape),
            whole(expand_w.shape),
        ],
        out_specs=[whole(shape) for shape, _ in shapes],
        out_shape=[jax.ShapeDtypeStruct(*shape) for shape in shapes],
        scratch_shapes=[
            pltpu.VMEM((3, area + 2 * line, channels), jnp.bfloat16),
            pltpu.VMEM((area, channels), jnp.float32),
        ],
        compiler_params=params(40),
        cost_estimate=pl.CostEstimate(
            flops=18 * area * channels * channels, bytes_accessed=9000000, transcendentals=area * channels
        ),
    )(cotangent, mixed, squeezed, gate, rows, reduce_w, expand_w)
    return d_in, parts


def weight_rows(images, d_mixed, tail, side, count):
    area, channels = images.shape
    line = side * count

    def body(x_ref, dm_ref, tail_ref, out_ref, shifted):
        step = pl.program_id(0)

        @pl.when(step == 0)
        def _():
            spread(x_ref[...].astype(jnp.float32), shifted, side, count)

        @pl.when(step < 9)
        def _():
            here = pl.ds(pl.multiple_of((step // 3) * line, line), area)
            out_ref[...] = lax.dot_general(
                shifted[step % 3, here, :],
                dm_ref[...],
                (((0,), (0,)), ((), ())),
                preferred_element_type=jnp.float32,
            ).astype(jnp.bfloat16)

        @pl.when(step == 9)
        def _():
            out_ref[...] = tail_ref[...]

    return pl.pallas_call(
        body,
        grid=(10,),
        in_specs=[whole(images.shape), whole(d_mixed.shape), whole(tail.shape)],
        out_specs=pl.BlockSpec((channels, channels), lambda step: (step, 0)),
        out_shape=jax.ShapeDtypeStruct((10 * channels, channels), jnp.bfloat16),
        scratch_shapes=[pltpu.VMEM((3, area + 2 * line, channels), jnp.bfloat16)],
        compiler_params=params(40),
        cost_estimate=pl.CostEstimate(
            flops=18 * area * channels * channels, bytes_accessed=7000000, transcendentals=0
        ),
    )(images, d_mixed, tail)


def transposed_dot(left, right):
    return lax.dot_general(
        left.astype(jnp.bfloat16),
        right.astype(jnp.bfloat16),
        (((0,), (0,)), ((), ())),
        preferred_element_type=jnp.float32,
    ).astype(jnp.bfloat16)


def per_device(student_in, teacher_in, out_grad, student_params, teacher_params):
    shape = student_in.shape
    channels, side, count = shape[-1], shape[2], shape[0] * shape[1]
    sections = lax.axis_size("segment")
    section = lax.axis_index("segment")

    def pack(array):
        array = array.reshape((count, side, side, channels)).transpose(1, 2, 0, 3)
        return array.reshape(side * side * count, channels)

    def unpack(array):
        array = array.reshape((side, side, count, channels)).transpose(2, 0, 1, 3)
        return array.reshape((1,) + shape)

    student_own = to_matrix(student_params, channels)
    student_rows = lax.all_gather(student_own, "dp", axis=0, tiled=True)
    teacher_own = to_matrix(teacher_params, channels)
    student_rows, teacher_own = lax.optimization_barrier((student_rows, teacher_own))
    teacher_rows = lax.all_gather(teacher_own, "dp", axis=0, tiled=True)
    student_w = split_rows(student_rows, channels, SE)

    current = pack(student_in)
    for step in range(sections):
        result, held = forward(current, *student_w, side, count)
        if step + 1 < sections:
            got = hop(result, "segment", step, step + 1)
            current = jnp.where(section == step + 1, got, current)

    grad = pack(out_grad)
    for step in range(sections):
        if step == sections // 2:
            grad, teacher_rows = lax.optimization_barrier((grad, teacher_rows))
        result, parts = pull_back(grad, *student_w, held, side, count)
        if step + 1 < sections:
            got = hop(result, "segment", sections - 1 - step, sections - 2 - step)
            grad = jnp.where(section == sections - 2 - step, got, grad)
    input_grads = result

    d_mixed, d_gate, d_squeezed = parts
    _, pooled, _, hidden, _ = held
    tail = jnp.concatenate(
        [
            transposed_dot(pooled, d_squeezed).reshape(-1, channels),
            transposed_dot(hidden, d_gate).reshape(-1, channels),
        ],
        axis=0,
    )
    rows = weight_rows(current, d_mixed, tail, side, count)
    grad_own = lax.psum_scatter(rows, "dp", scatter_dimension=0, tiled=True)

    teacher_w = split_rows(teacher_rows, channels, SE)
    teacher_now, _ = lax.optimization_barrier((pack(teacher_in), rows))
    for step in range(sections):
        teacher_out, _ = forward(teacher_now, *teacher_w, side, count)
        if step + 1 < sections:
            got = hop(teacher_out, "segment", step, step + 1)
            teacher_now = jnp.where(section == step + 1, got, teacher_now)

    grad_shard, teacher_new = finish(grad_own, student_params, teacher_params)
    return (unpack(teacher_out), unpack(input_grads), grad_shard, teacher_new)


def solution(mesh):
    placed = (
        P(None, "dp", None, None, None),
        P(None, "dp", None, None, None),
        P(None, "dp", None, None, None),
        P("segment", "dp"),
        P("segment", "dp"),
    )
    return jax.shard_map(
        per_device,
        mesh=mesh,
        in_specs=placed,
        out_specs=(
            P("segment", None, "dp", None, None, None),
            P("segment", None, "dp", None, None, None),
            P("segment", "dp"),
            P("segment", "dp"),
        ),
        check_vma=False,
    )
```

time: 442 us -> 326 us (0.74); the launches traced: 437 us -> 326 us
  matrix products: 85.9 us -> 0.53 us
  Pallas kernels: 0 us -> 67.2 us
  other arithmetic: 58.9 us -> 1.66 us
  starting transfers between devices: 39 us -> 8.31 us
    dot_general x29 -> x2, matrix products: 85.9 us -> 0.53 us  [transposed_dot(): lax.dot_general(left.astype(jnp.bfloat16), right.astype(jnp.bfloat16), ((...]
    pallas_call x0 -> x16, Pallas kernels: none -> 67.2 us  [the longest x8 39.2 us: forward(): pl.pallas_call(body, grid=(3,), in_specs=[whole(images.shape), pl.BlockSp...]
    ppermute x9, starting transfers between devices: 38.6 us -> 8.19 us  [hop(): return lax.ppermute(array, axis, [(source, target)])]
    ppermute x9, waiting for transfers between devices: 33.1 us -> 5.61 us  [hop(): return lax.ppermute(array, axis, [(source, target)])]
    convert_element_type x17 -> x0, other arithmetic: 26.1 us -> none  [the longest x1 14.7 us: per_device(): student_own.astype(jnp.bfloat16)]
    reduce_scatter x1, waiting for transfers between devices: 51.9 us -> 70.2 us  [per_device(): grad_own = lax.psum_scatter(rows, 'dp', scatter_dimension=0, tiled=True)]
    unnamed x5 -> x0, other arithmetic: 14.2 us -> none
    concatenate x1, other arithmetic: 11.7 us -> 0.04 us  [per_device(): jnp.concatenate([transposed_dot(pooled, d_squeezed).reshape(-1, channels)...]
  transfers between devices with their start and end apart: 12 -> 12, of which waited for: 10 -> 6; matrix products, arithmetic and copies ran while one was open for 20% -> 2% of each run, Pallas kernels for 0% -> 15%
where the time goes in v2:
time: 326 us
  waiting for transfers between devices  203 us (62%)
  Pallas kernels  67.2 us (21%)
  local copies, waits for them, and re-layouts  30.5 us (9%)
  between operations  14.2 us (4%)
  starting transfers between devices  8.31 us (3%)
    all_gather x1, waiting for transfers between devices, per_device(): student_rows = lax.all_gather(student_own, 'dp', axis=0, tiled=True)  87.9 us
    reduce_scatter x1, waiting for transfers between devices, per_device(): grad_own = lax.psum_scatter(rows, 'dp', scatter_dimension=0, tiled=True)  70.2 us
    all_gather x1, waiting for transfers between devices, per_device(): teacher_rows = lax.all_gather(teacher_own, 'dp', axis=0, tiled=True)  39.6 us
    pallas_call x8, Pallas kernels, forward(): pl.pallas_call(body, grid=(3,), in_specs=[whole(images.shape), pl.BlockSp...  39.2 us
    unnamed x36, local copies, waits for them, and re-layouts  25.4 us
    pallas_call x4, Pallas kernels, pull_back(): pl.pallas_call(body, grid=(3,), in_specs=[whole(cotangent.shape), whole(m...  19.4 us
    ppermute x9, starting transfers between devices, hop(): return lax.ppermute(array, axis, [(source, target)])  8.19 us
  transfers between devices with their start and end apart: 12, of which 6 were waited for; matrix products, arithmetic and copies ran while one was open for 2% of the time, Pallas kernels for 15%

profile of v2, /device:TPU:0, one launch (start us, length us, event | category | flops | bytes accessed | tf_op | source)
XLA Modules:
  0.0 325.7 jit_solution(8409834469086780941)
XLA Ops:
  7.2 1.3 copy-done.1
  8.5 1.0 shard_map.84
  9.6 1.3 copy-done.3
  10.9 1.0 shard_map.85
  11.9 87.9 %all-gather.3.cloned.1.call-done.kernel_ref = bf16[5120,512]{1,0:T(8,128)(2,1)} async-done(((bf16[640,512]{1,0:T(8,128)(2,1)}), bf16[5120,512]{1,0:T(8,128)(2,1)}) %all-gather.3.cloned.1.call-update) | async-done | bytes 5242896 | tf_op jit(solution)/shard_map/all_gather | solution.py:330
  100.1 1.1 fusion.5
  101.3 2.5 copy-done.7
  103.8 4.9 %shard_map.86 = (bf16[512,512]{1,0:T(8,128)(2,1)S(1)}, f32[512,512]{1,0:T(8,128)}, f32[8,512]{1,0:T(8,128)}, f32[8,256]{1,0:T(8,128)}, f32[8,256]{1,0:T(8,128)}, /*index=5*/f32[8,512]{1,0:T(8,128)}) custom-call(bf16[512,512]{1,0:T(8,128)(2,1)S(1)} %bitcast.30, bf16[5120,512]{1,0:T(8,128)(2,1)S(1)} %copy-done.7, bf16[512,256]{1,0:T(8,128)(2,1)S(1)} %reshape.67.red_ref, ...), custom_call_target="tpu_custom_call" | custom-call | flops 2415919104 | bytes 8000000 | tf_op jit(solution)/shard_map/pallas_call | solution.py:161
  108.7 1.3 collective-permute-start
  110.0 1.5 collective-permute-done
  111.6 2.5 copy-done.8
  114.1 4.9 %shard_map.87 = (bf16[512,512]{1,0:T(8,128)(2,1)S(1)}, f32[512,512]{1,0:T(8,128)}, f32[8,512]{1,0:T(8,128)}, f32[8,256]{1,0:T(8,128)}, f32[8,256]{1,0:T(8,128)}, /*index=5*/f32[8,512]{1,0:T(8,128)}) custom-call(bf16[512,512]{1,0:T(8,128)(2,1)S(1)} %broadcast_select_fusion.3.x_ref, bf16[5120,512]{1,0:T(8,128)(2,1)S(1)} %copy-done.8, ...), custom_call_target="tpu_custom_call" | custom-call | flops 2415919104 | bytes 8000000 | tf_op jit(solution)/shard_map/pallas_call | solution.py:161
  119.0 0.7 collective-permute-start.1
  119.8 2.5 copy-done.9
  122.3 4.9 %shard_map.88 = (bf16[512,512]{1,0:T(8,128)(2,1)S(1)}, f32[512,512]{1,0:T(8,128)}, f32[8,512]{1,0:T(8,128)}, f32[8,256]{1,0:T(8,128)}, f32[8,256]{1,0:T(8,128)}, /*index=5*/f32[8,512]{1,0:T(8,128)}) custom-call(bf16[512,512]{1,0:T(8,128)(2,1)S(1)} %broadcast_select_fusion.6.x_ref, bf16[5120,512]{1,0:T(8,128)(2,1)S(1)} %copy-done.9, ...), custom_call_target="tpu_custom_call" | custom-call | flops 2415919104 | bytes 8000000 | tf_op jit(solution)/shard_map/pallas_call | solution.py:161
  127.3 0.7 collective-permute-start.2
  128.4 2.5 copy-done.10
  130.8 4.7 %shard_map.89 = (bf16[512,512]{1,0:T(8,128)(2,1)}, f32[512,512]{1,0:T(8,128)S(1)}, f32[8,512]{1,0:T(8,128)S(1)}, f32[8,256]{1,0:T(8,128)S(1)}, f32[8,256]{1,0:T(8,128)S(1)}, /*index=5*/f32[8,512]{1,0:T(8,128)S(1)}) custom-call(bf16[512,512]{1,0:T(8,128)(2,1)S(1)} %broadcast_select_fusion.8.x_ref, bf16[5120,512]{1,0:T(8,128)(2,1)S(1)} %copy-done.10, ...), custom_call_target="tpu_custom_call" | custom-call | flops 2415919104 | bytes 8000000 | tf_op jit(solution)/shard_map/pallas_call | solution.py:161
  135.6 5.0 %shard_map.90 = (bf16[512,512]{1,0:T(8,128)(2,1)S(1)}, bf16[512,512]{1,0:T(8,128)(2,1)}, f32[8,512]{1,0:T(8,128)}, f32[8,256]{1,0:T(8,128)}) custom-call(bf16[512,512]{1,0:T(8,128)(2,1)S(1)} %bitcast.31, f32[512,512]{1,0:T(8,128)S(1)} %get-tuple-element.34.mixed_ref, f32[8,256]{1,0:T(8,128)S(1)} %get-tuple-element.35.sq_ref, ...), custom_call_target="tpu_custom_call" | custom-call | flops 2415919104 | bytes 9000000 | tf_op jit(solution)/shard_map/pallas_call | solution.py:241
  141.4 5.1 %shard_map.91 = (bf16[512,512]{1,0:T(8,128)(2,1)S(1)}, bf16[512,512]{1,0:T(8,128)(2,1)}, f32[8,512]{1,0:T(8,128)}, f32[8,256]{1,0:T(8,128)}) custom-call(bf16[512,512]{1,0:T(8,128)(2,1)S(1)} %broadcast_select_fusion.5.g_ref, f32[512,512]{1,0:T(8,128)S(1)} %get-tuple-element.34.mixed_ref, f32[8,256]{1,0:T(8,128)S(1)} %get-tuple-element.35.sq_ref, ...), custom_call_target="tpu_custom_call" | custom-call | flops 2415919104 | bytes 9000000 | tf_op jit(solution)/shard_map/pallas_call | solution.py:241
  146.5 0.9 collective-permute-start.4
  147.4 39.6 %all-gather.5.cloned.1.call-done.kernel_ref = bf16[5120,512]{1,0:T(8,128)(2,1)} async-done(((bf16[640,512]{1,0:T(8,128)(2,1)}), bf16[5120,512]{1,0:T(8,128)(2,1)}) %all-gather.5.cloned.1.call-update) | async-done | bytes 5242896 | tf_op jit(solution)/shard_map/all_gather | solution.py:333
  187.0 2.5 copy-done.11
  189.5 5.0 %shard_map.92 = (bf16[512,512]{1,0:T(8,128)(2,1)S(1)}, bf16[512,512]{1,0:T(8,128)(2,1)}, f32[8,512]{1,0:T(8,128)}, f32[8,256]{1,0:T(8,128)}) custom-call(bf16[512,512]{1,0:T(8,128)(2,1)S(1)} %broadcast_select_fusion.2.g_ref, f32[512,512]{1,0:T(8,128)S(1)} %get-tuple-element.34.mixed_ref, f32[8,256]{1,0:T(8,128)S(1)} %get-tuple-element.35.sq_ref, ...), custom_call_target="tpu_custom_call" | custom-call | flops 2415919104 | bytes 9000000 | tf_op jit(solution)/shard_map/pallas_call | solution.py:241
  194.5 1.3 collective-permute-start.5
  195.8 2.6 collective-permute-done.5
  198.4 1.1 broadcast_select_fusion.g_ref
  199.6 2.5 copy-done.12
  202.0 4.2 %shard_map.93 = (bf16[512,512]{1,0:T(8,128)(2,1)S(1)}, bf16[512,512]{1,0:T(8,128)(2,1)S(1)}, f32[8,512]{1,0:T(8,128)S(1)}, f32[8,256]{1,0:T(8,128)S(1)}) custom-call(bf16[512,512]{1,0:T(8,128)(2,1)S(1)} %broadcast_select_fusion.g_ref, f32[512,512]{1,0:T(8,128)S(1)} %get-tuple-element.34.mixed_ref, f32[8,256]{1,0:T(8,128)S(1)} %get-tuple-element.35.sq_ref, ...), custom_call_target="tpu_custom_call" | custom-call | flops 2415919104 | bytes 9000000 | tf_op jit(solution)/shard_map/pallas_call | solution.py:241
  206.3 0.8 copy-done.13
  207.8 1.0 copy-done.14
  208.8 4.6 %shard_map.94 = bf16[5120,512]{1,0:T(8,128)(2,1)S(1)} custom-call(bf16[512,512]{1,0:T(8,128)(2,1)S(1)} %broadcast_select_fusion.8.x_ref, bf16[512,512]{1,0:T(8,128)(2,1)S(1)} %copy-done.14, bf16[512,512]{1,0:T(8,128)(2,1)S(1)} %pad_maximum_fusion.tail_ref), custom_call_target="tpu_custom_call" | custom-call | flops 2415919104 | bytes 7000000 | tf_op jit(solution)/shard_map/pallas_call | solution.py:292
  213.4 2.4 copy-done
  216.1 1.1 fusion.4
  217.3 2.5 copy-done.6
  219.8 4.9 %shard_map.95 = (bf16[512,512]{1,0:T(8,128)(2,1)S(1)}, f32[512,512]{1,0:T(8,128)}, f32[8,512]{1,0:T(8,128)}, f32[8,256]{1,0:T(8,128)}, f32[8,256]{1,0:T(8,128)}, /*index=5*/f32[8,512]{1,0:T(8,128)}) custom-call(bf16[512,512]{1,0:T(8,128)(2,1)S(1)} %bitcast.32, bf16[5120,512]{1,0:T(8,128)(2,1)S(1)} %copy-done.6, bf16[512,256]{1,0:T(8,128)(2,1)S(1)} %reshape.71.red_ref, ...), custom_call_target="tpu_custom_call" | custom-call | flops 2415919104 | bytes 8000000 | tf_op jit(solution)/shard_map/pallas_call | solution.py:161
  224.7 1.3 collective-permute-start.6
  226.0 1.5 collective-permute-done.6
  227.6 4.9 %shard_map.96 = (bf16[512,512]{1,0:T(8,128)(2,1)S(1)}, f32[512,512]{1,0:T(8,128)}, f32[8,512]{1,0:T(8,128)}, f32[8,256]{1,0:T(8,128)}, f32[8,256]{1,0:T(8,128)}, /*index=5*/f32[8,512]{1,0:T(8,128)}) custom-call(bf16[512,512]{1,0:T(8,128)(2,1)S(1)} %broadcast_select_fusion.1.x_ref, bf16[5120,512]{1,0:T(8,128)(2,1)S(1)} %copy-done.6, ...), custom_call_target="tpu_custom_call" | custom-call | flops 2415919104 | bytes 8000000 | tf_op jit(solution)/shard_map/pallas_call | solution.py:161
  232.5 0.7 collective-permute-start.7
  233.3 4.9 %shard_map.97 = (bf16[512,512]{1,0:T(8,128)(2,1)S(1)}, f32[512,512]{1,0:T(8,128)}, f32[8,512]{1,0:T(8,128)}, f32[8,256]{1,0:T(8,128)}, f32[8,256]{1,0:T(8,128)}, /*index=5*/f32[8,512]{1,0:T(8,128)}) custom-call(bf16[512,512]{1,0:T(8,128)(2,1)S(1)} %broadcast_select_fusion.4.x_ref, bf16[5120,512]{1,0:T(8,128)(2,1)S(1)} %copy-done.6, ...), custom_call_target="tpu_custom_call" | custom-call | flops 2415919104 | bytes 8000000 | tf_op jit(solution)/shard_map/pallas_call | solution.py:161
  238.2 0.7 collective-permute-start.8
  238.9 0.9 copy.13
  239.9 4.9 %shard_map.98 = (bf16[512,512]{1,0:T(8,128)(2,1)S(1)}, f32[512,512]{1,0:T(8,128)}, f32[8,512]{1,0:T(8,128)}, f32[8,256]{1,0:T(8,128)}, f32[8,256]{1,0:T(8,128)}, /*index=5*/f32[8,512]{1,0:T(8,128)}) custom-call(bf16[512,512]{1,0:T(8,128)(2,1)S(1)} %broadcast_select_fusion.7.x_ref, bf16[5120,512]{1,0:T(8,128)(2,1)S(1)} %copy-done.6, ...), custom_call_target="tpu_custom_call" | custom-call | flops 2415919104 | bytes 8000000 | tf_op jit(solution)/shard_map/pallas_call | solution.py:161
  244.9 0.9 copy.12
  245.8 70.2 %reduce-scatter.2.cloned.1.call-done.grad_ref = bf16[640,512]{1,0:T(8,128)(2,1)} async-done(((bf16[5120,512]{1,0:T(8,128)(2,1)}), bf16[640,512]{1,0:T(8,128)(2,1)}) %reduce-scatter.2.cloned.1.call-update) | async-done | bytes 655376 | tf_op jit(solution)/shard_map/reduce_scatter | solution.py:363
  316.0 1.1 copy-done.5
  317.1 2.1 shard_map.99
  (53 shorter events, 3.2 us)
Async XLA Ops:
  7.2 92.6 %all-gather.3.cloned.1.call-start = ((), (), s32[]{:S(2)}) async-start(), calls=%async_computation.1 | async-start | bytes 5898240 | tf_op jit(solution)/shard_map/all_gather | solution.py:330
  7.2 1.3 copy-start.1
  8.5 91.3 %copy-start.15 = (bf16[4,2,8,8,512]{4,3,2,1,0:T(8,128)(2,1)S(1)}, bf16[4,2,8,8,512]{4,3,2,1,0:T(8,128)(2,1)}, u32[]{:S(2)}) copy-start(bf16[4,2,8,8,512]{4,3,2,1,0:T(8,128)(2,1)} %param.5) | copy-start | bytes 1572868
  9.5 177.5 %all-gather.5.cloned.1.call-start = ((), (), s32[]{:S(2)}) async-start(), calls=%async_computation.2 | async-start | bytes 5898240 | tf_op jit(solution)/shard_map/all_gather | solution.py:333
  9.6 1.3 copy-start.3
  99.8 216.2 %reduce-scatter.2.cloned.1.call-start = ((), (), s32[]{:S(2)}) async-start(), calls=%async_computation.3 | async-start | bytes 5898240 | tf_op jit(solution)/shard_map/reduce_scatter | solution.py:363
  101.3 2.5 copy-start.7
  108.7 2.8 collective-permute-start
  111.6 2.5 copy-start.8
  119.0 0.7 collective-permute-start.1
  119.7 8.3 %copy-start.16 = (bf16[4,2,8,8,512]{4,3,2,1,0:T(8,128)(2,1)S(1)}, bf16[4,2,8,8,512]{4,3,2,1,0:T(8,128)(2,1)}, u32[]{:S(2)}) copy-start(bf16[4,2,8,8,512]{4,3,2,1,0:T(8,128)(2,1)} %param.7) | copy-start | bytes 1572868
  119.8 2.6 copy-start.9
  127.3 1.0 collective-permute-start.2
  128.3 2.5 copy-start.10
  140.6 0.7 collective-permute-start.3
  146.5 0.9 collective-permute-start.4
  187.0 2.5 copy-start.11
  194.5 3.9 %collective-permute-start.5 = (bf16[512,512]{1,0:T(8,128)(2,1)S(1)}, bf16[512,512]{1,0:T(8,128)(2,1)}, u32[]{:S(2)}, u32[]{:S(2)}) collective-permute-start(bf16[512,512]{1,0:T(8,128)(2,1)S(1)} %get-tuple-element.41), channel_id=1, source_target_pairs={{8,0},{9,1},{10,2},{11,3},{12,4},{13,5},{14,6},{15,7}} | collective-permute-start | bytes 1572872 | tf_op jit(solution)/shard_map/ppermute | solution.py:16
  199.5 2.5 copy-start.12
  206.3 0.8 copy-start.13
  207.8 1.0 copy-start.14
  208.8 7.0 %copy-start.17 = (bf16[4,2,8,8,512]{4,3,2,1,0:T(8,128)(2,1)S(1)}, bf16[4,2,8,8,512]{4,3,2,1,0:T(8,128)(2,1)}, u32[]{:S(2)}) copy-start(bf16[4,2,8,8,512]{4,3,2,1,0:T(8,128)(2,1)} %param.6) | copy-start | bytes 1572868
  213.4 2.4 copy-start
  217.3 2.5 copy-start.6
  224.7 2.8 collective-permute-start.6
  232.5 0.7 collective-permute-start.7
  238.2 1.6 collective-permute-start.8
  239.9 76.1 %copy-start.2 = (f32[1,327680]{1,0:T(1,128)S(1)}, f32[1,327680]{1,0:T(1,128)}, u32[]{:S(2)}) copy-start(f32[1,327680]{1,0:T(1,128)} %param.8) | copy-start | bytes 3932164
  239.9 76.1 %copy-start.4 = (f32[1,327680]{1,0:T(1,128)S(1)}, f32[1,327680]{1,0:T(1,128)}, u32[]{:S(2)}) copy-start(f32[1,327680]{1,0:T(1,128)} %param.9) | copy-start | bytes 3932164
  316.0 1.1 copy-start.5
Sparse Core Ops, SparseCore 0:
  10.8 88.9 all-gather.2
  102.5 84.4 all-gather.4
  215.9 100.0 reduce-scatter.1

commit v3 on v2

--- a/solution.py
+++ b/solution.py
@@ -303,6 +303,127 @@
     )(images, d_mixed, tail)
 
 
+def ring_sizes():
+    across = max(lax.axis_size("segment") // 2, 1)
+    return across, lax.axis_size("dp") // across
+
+
+def ring_place(spot):
+    across, along = ring_sizes()
+    if across == 1:
+        return spot
+    away = (spot // along + across - 1) // across
+    rest = away * (spot - along)
+    row, step = rest // (across - 1), rest % (across - 1)
+    x = 1 + step + (row % 2) * (across - 2 - 2 * step)
+    return (1 - away) * spot * across + away * ((along - 1 - row) * across + x)
+
+
+def ring_spot(place):
+    across, along = ring_sizes()
+    if across == 1:
+        return place
+    x, z = place % across, place // across
+    away = (x + across - 1) // across
+    row = along - 1 - z
+    step = x - 1 + (row % 2) * (across - 2 - 2 * (x - 1))
+    return (1 - away) * z + away * (along + row * (across - 1) + step)
+
+
+def ring_gather(own):
+    peers = lax.axis_size("dp")
+    depth, channels = own.shape
+    half = depth // 2
+    pieces = 2 if half % 32 == 0 else 1
+    part = half // pieces
+    lanes = [(way, piece) for piece in range(pieces) for way in range(2)]
+
+    def body(own_ref, out_ref, local_sem, send_sem, recv_sem):
+        me = lax.axis_index("dp")
+        spot = ring_spot(me)
+        sides = (ring_place((spot + 1) % peers), ring_place((spot + peers - 1) % peers))
+        barrier = pltpu.get_barrier_semaphore()
+        for side in sides:
+            pl.semaphore_signal(
+                barrier, inc=1, device_id={"dp": side}, device_id_type=pl.DeviceIdType.MESH
+            )
+        pl.semaphore_wait(barrier, 2)
+
+        def copy(step, way, piece):
+            spot_of = spot + peers - step if way == 0 else spot + step
+            start = way * half + piece * part
+            block = pl.multiple_of(ring_place(spot_of % peers) * depth, 16)
+            landing = out_ref.at[pl.ds(block + start, part)]
+            source = own_ref.at[pl.ds(start, part)] if step == 0 else landing
+            return pltpu.make_async_remote_copy(
+                src_ref=source,
+                dst_ref=landing,
+                send_sem=send_sem.at[way, piece, step],
+                recv_sem=recv_sem.at[way, piece, step],
+                device_id={"dp": sides[way]},
+                device_id_type=pl.DeviceIdType.MESH,
+            )
+
+        copies = {}
+        for step in range(peers - 1):
+            for way, piece in lanes:
+                if step > 0:
+                    copies[step - 1, way, piece].wait_recv()
+                copies[step, way, piece] = copy(step, way, piece)
+                copies[step, way, piece].start()
+            if step == 0:
+                mine = pltpu.make_async_copy(
+                    own_ref, out_ref.at[pl.ds(pl.multiple_of(me * depth, 16), depth)], local_sem
+                )
+                mine.start()
+        for way, piece in lanes:
+            copies[peers - 2, way, piece].wait_recv()
+        for key in copies:
+            copies[key].wait_send()
+        mine.wait()
+
+    return pl.pallas_call(
+        body,
+        in_specs=[pl.BlockSpec(memory_space=pl.ANY)],
+        out_specs=pl.BlockSpec(memory_space=pl.ANY),
+        out_shape=jax.ShapeDtypeStruct((peers * depth, channels), own.dtype),
+        scratch_shapes=[
+            pltpu.SemaphoreType.DMA,
+            pltpu.SemaphoreType.DMA((2, pieces, peers - 1)),
+            pltpu.SemaphoreType.DMA((2, pieces, peers - 1)),
+        ],
+        compiler_params=pltpu.CompilerParams(collective_id=0, has_side_effects=True),
+        cost_estimate=pl.CostEstimate(
+            flops=0, bytes_accessed=4 * peers * depth * channels, transcendentals=0
+        ),
+    )(own)
+
+
+def ring_scatter(rows):
+    peers = lax.axis_size("dp")
+    depth = rows.shape[0] // peers
+    half = depth // 2
+    spot = ring_spot(lax.axis_index("dp"))
+    order = [ring_place(at) for at in range(peers)]
+    pairs = (
+        [(order[at], order[(at + 1) % peers]) for at in range(peers)],
+        [(order[(at + 1) % peers], order[at]) for at in range(peers)],
+    )
+
+    def term(way, step):
+        spot_of = spot + 2 * peers - 1 - step if way == 0 else spot + 1 + step
+        start = ring_place(spot_of % peers) * depth + way * half
+        return lax.dynamic_slice_in_dim(rows, start, half, 0)
+
+    moving = [term(way, 0) for way in range(2)]
+    for step in range(peers - 1):
+        for way in range(2):
+            got = lax.ppermute(moving[way], "dp", pairs[way])
+            total = got.astype(jnp.float32) + term(way, step + 1).astype(jnp.float32)
+            moving[way] = total if step == peers - 2 else total.astype(jnp.bfloat16)
+    return jnp.concatenate(moving, axis=0)
+
+
 def transposed_dot(left, right):
     return lax.dot_general(
         left.astype(jnp.bfloat16),
@@ -327,7 +448,7 @@
         return array.reshape((1,) + shape)
 
     student_own = to_matrix(student_params, channels)
-    student_rows = lax.all_gather(student_own, "dp", axis=0, tiled=True)
+    student_rows = ring_gather(student_own)
     teacher_own = to_matrix(teacher_params, channels)
     student_rows, teacher_own = lax.optimization_barrier((student_rows, teacher_own))
     teacher_rows = lax.all_gather(teacher_own, "dp", axis=0, tiled=True)
@@ -342,13 +463,12 @@
 
     grad = pack(out_grad)
     for step in range(sections):
-        if step == sections // 2:
-            grad, teacher_rows = lax.optimization_barrier((grad, teacher_rows))
         result, parts = pull_back(grad, *student_w, held, side, count)
         if step + 1 < sections:
             got = hop(result, "segment", sections - 1 - step, sections - 2 - step)
             grad = jnp.where(section == sections - 2 - step, got, grad)
     input_grads = result
+    parts[0], teacher_rows = lax.optimization_barrier((parts[0], teacher_rows))
 
     d_mixed, d_gate, d_squeezed = parts
     _, pooled, _, hidden, _ = held
@@ -360,7 +480,7 @@
         axis=0,
     )
     rows = weight_rows(current, d_mixed, tail, side, count)
-    grad_own = lax.psum_scatter(rows, "dp", scatter_dimension=0, tiled=True)
+    grad_own = ring_scatter(rows)
 
     teacher_w = split_rows(teacher_rows, channels, SE)
     teacher_now, _ = lax.optimization_barrier((pack(teacher_in), rows))

time: 326 us -> 260 us (0.80)
  waiting for transfers between devices: 203 us -> 42.9 us
  Pallas kernels: 67.2 us -> 121 us
  starting transfers between devices: 8.31 us -> 26.2 us
  other arithmetic: 1.66 us -> 16.7 us
  local copies, waits for them, and re-layouts: 30.5 us -> 37.1 us
    all_gather x1 -> x0, waiting for transfers between devices: 87.9 us -> none  [per_device(): student_rows = lax.all_gather(student_own, 'dp', axis=0, tiled=True)]
    reduce_scatter x1 -> x0, waiting for transfers between devices: 70.2 us -> none  [per_device(): grad_own = lax.psum_scatter(rows, 'dp', scatter_dimension=0, tiled=True)]
    pallas_call x0 -> x1, Pallas kernels: none -> 55 us  [ring_gather(): pl.pallas_call(body, in_specs=[pl.BlockSpec(memory_space=pl.ANY)], out_sp...]
    all_gather x1, waiting for transfers between devices: 39.6 us -> 0.02 us  [per_device(): teacher_rows = lax.all_gather(teacher_own, 'dp', axis=0, tiled=True)]
    ppermute x0 -> x14, waiting for transfers between devices: none -> 19 us  [ring_scatter(): got = lax.ppermute(moving[way], 'dp', pairs[way])]
    ppermute x9, waiting for transfers between devices: 5.61 us -> 23.8 us  [hop(): return lax.ppermute(array, axis, [(source, target)])]
    ppermute x0 -> x14, starting transfers between devices: none -> 14.2 us  [ring_scatter(): got = lax.ppermute(moving[way], 'dp', pairs[way])]
    convert_element_type x0 -> x6, other arithmetic: none -> 12.7 us  [ring_scatter(): moving[way] = total if step == peers - 2 else total.astype(jnp.bfloat16)]
  transfers between devices with their start and end apart: 12 -> 24, of which waited for: 6 -> 8; matrix products, arithmetic and copies ran while one was open for 2% -> 7% of each run, Pallas kernels for 15% -> 23%
where the time goes in v3:
time: 260 us; the launch traced here: 259 us
  Pallas kernels  121 us (47%)
  waiting for transfers between devices  42.9 us (16%)
  local copies, waits for them, and re-layouts  37.1 us (14%)
  starting transfers between devices  26.2 us (10%)
  other arithmetic  16.7 us (6%)
  between operations  14.6 us (6%)
    pallas_call x1, Pallas kernels, ring_gather(): pl.pallas_call(body, in_specs=[pl.BlockSpec(memory_space=pl.ANY)], out_sp...  55 us
    pallas_call x8, Pallas kernels, forward(): pl.pallas_call(body, grid=(3,), in_specs=[whole(images.shape), pl.BlockSp...  39.1 us
    unnamed x34, local copies, waits for them, and re-layouts  28.2 us
    ppermute x9, waiting for transfers between devices, hop(): return lax.ppermute(array, axis, [(source, target)])  23.8 us
    pallas_call x4, Pallas kernels, pull_back(): pl.pallas_call(body, grid=(3,), in_specs=[whole(cotangent.shape), whole(m...  19.4 us
    ppermute x14, waiting for transfers between devices, ring_scatter(): got = lax.ppermute(moving[way], 'dp', pairs[way])  19 us
    ppermute x14, starting transfers between devices, ring_scatter(): got = lax.ppermute(moving[way], 'dp', pairs[way])  14.2 us
    convert_element_type x6, other arithmetic, ring_scatter(): moving[way] = total if step == peers - 2 else total.astype(jnp.bfloat16)  12.7 us
  transfers between devices with their start and end apart: 24, of which 8 were waited for; matrix products, arithmetic and copies ran while one was open for 7% of the time, Pallas kernels for 23%

profile of v3, /device:TPU:0, one launch (start us, length us, event | category | flops | bytes accessed | tf_op | source)
XLA Modules:
  0.0 259.3 jit_solution(5427953430131436932)
XLA Ops:
  7.2 1.4 copy-done.7
  9.6 55.0 %shard_map.85.kernel_ref = bf16[5120,512]{1,0:T(8,128)(2,1)} custom-call(bf16[640,512]{1,0:T(8,128)(2,1)} %copy-done.9), custom_call_target="tpu_custom_call" | custom-call | bytes 10485760 | tf_op jit(solution)/shard_map/pallas_call | solution.py:385
  67.2 2.5 copy-done
  69.6 4.9 %shard_map.87 = (bf16[512,512]{1,0:T(8,128)(2,1)S(1)}, f32[512,512]{1,0:T(8,128)}, f32[8,512]{1,0:T(8,128)}, f32[8,256]{1,0:T(8,128)}, f32[8,256]{1,0:T(8,128)}, /*index=5*/f32[8,512]{1,0:T(8,128)}) custom-call(bf16[512,512]{1,0:T(8,128)(2,1)S(1)} %bitcast.32, bf16[5120,512]{1,0:T(8,128)(2,1)S(1)} %copy-done, bf16[512,256]{1,0:T(8,128)(2,1)S(1)} %reshape.67.red_ref, ...), custom_call_target="tpu_custom_call" | custom-call | flops 2415919104 | bytes 8000000 | tf_op jit(solution)/shard_map/pallas_call | solution.py:161
  75.9 1.5 collective-permute-done
  77.5 2.5 copy-done.1
  79.9 4.9 %shard_map.88 = (bf16[512,512]{1,0:T(8,128)(2,1)S(1)}, f32[512,512]{1,0:T(8,128)}, f32[8,512]{1,0:T(8,128)}, f32[8,256]{1,0:T(8,128)}, f32[8,256]{1,0:T(8,128)}, /*index=5*/f32[8,512]{1,0:T(8,128)}) custom-call(bf16[512,512]{1,0:T(8,128)(2,1)S(1)} %broadcast_select_fusion.3.x_ref, bf16[5120,512]{1,0:T(8,128)(2,1)S(1)} %copy-done.1, ...), custom_call_target="tpu_custom_call" | custom-call | flops 2415919104 | bytes 8000000 | tf_op jit(solution)/shard_map/pallas_call | solution.py:161
  84.9 1.4 collective-permute-start.1
  86.4 2.5 copy-done.2
  88.9 4.9 %shard_map.89 = (bf16[512,512]{1,0:T(8,128)(2,1)S(1)}, f32[512,512]{1,0:T(8,128)}, f32[8,512]{1,0:T(8,128)}, f32[8,256]{1,0:T(8,128)}, f32[8,256]{1,0:T(8,128)}, /*index=5*/f32[8,512]{1,0:T(8,128)}) custom-call(bf16[512,512]{1,0:T(8,128)(2,1)S(1)} %broadcast_select_fusion.6.x_ref, bf16[5120,512]{1,0:T(8,128)(2,1)S(1)} %copy-done.2, ...), custom_call_target="tpu_custom_call" | custom-call | flops 2415919104 | bytes 8000000 | tf_op jit(solution)/shard_map/pallas_call | solution.py:161
  93.8 1.4 collective-permute-start.2
  96.7 2.5 copy-done.3
  99.1 4.7 %shard_map.90 = (bf16[512,512]{1,0:T(8,128)(2,1)}, f32[512,512]{1,0:T(8,128)S(1)}, f32[8,512]{1,0:T(8,128)S(1)}, f32[8,256]{1,0:T(8,128)S(1)}, f32[8,256]{1,0:T(8,128)S(1)}, /*index=5*/f32[8,512]{1,0:T(8,128)S(1)}) custom-call(bf16[512,512]{1,0:T(8,128)(2,1)S(1)} %broadcast_select_fusion.8.x_ref, bf16[5120,512]{1,0:T(8,128)(2,1)S(1)} %copy-done.3, ...), custom_call_target="tpu_custom_call" | custom-call | flops 2415919104 | bytes 8000000 | tf_op jit(solution)/shard_map/pallas_call | solution.py:161
  103.8 5.0 %shard_map.91 = (bf16[512,512]{1,0:T(8,128)(2,1)S(1)}, bf16[512,512]{1,0:T(8,128)(2,1)}, f32[8,512]{1,0:T(8,128)}, f32[8,256]{1,0:T(8,128)}) custom-call(bf16[512,512]{1,0:T(8,128)(2,1)S(1)} %bitcast.33, f32[512,512]{1,0:T(8,128)S(1)} %get-tuple-element.34.mixed_ref, f32[8,256]{1,0:T(8,128)S(1)} %get-tuple-element.35.sq_ref, ...), custom_call_target="tpu_custom_call" | custom-call | flops 2415919104 | bytes 9000000 | tf_op jit(solution)/shard_map/pallas_call | solution.py:241
  109.7 5.0 %shard_map.92 = (bf16[512,512]{1,0:T(8,128)(2,1)S(1)}, bf16[512,512]{1,0:T(8,128)(2,1)}, f32[8,512]{1,0:T(8,128)}, f32[8,256]{1,0:T(8,128)}) custom-call(bf16[512,512]{1,0:T(8,128)(2,1)S(1)} %broadcast_select_fusion.5.g_ref, f32[512,512]{1,0:T(8,128)S(1)} %get-tuple-element.34.mixed_ref, f32[8,256]{1,0:T(8,128)S(1)} %get-tuple-element.35.sq_ref, ...), custom_call_target="tpu_custom_call" | custom-call | flops 2415919104 | bytes 9000000 | tf_op jit(solution)/shard_map/pallas_call | solution.py:241
  115.7 5.0 %shard_map.93 = (bf16[512,512]{1,0:T(8,128)(2,1)S(1)}, bf16[512,512]{1,0:T(8,128)(2,1)}, f32[8,512]{1,0:T(8,128)}, f32[8,256]{1,0:T(8,128)}) custom-call(bf16[512,512]{1,0:T(8,128)(2,1)S(1)} %broadcast_select_fusion.2.g_ref, f32[512,512]{1,0:T(8,128)S(1)} %get-tuple-element.34.mixed_ref, f32[8,256]{1,0:T(8,128)S(1)} %get-tuple-element.35.sq_ref, ...), custom_call_target="tpu_custom_call" | custom-call | flops 2415919104 | bytes 9000000 | tf_op jit(solution)/shard_map/pallas_call | solution.py:241
  122.2 22.3 %collective-permute-done.5 = bf16[512,512]{1,0:T(8,128)(2,1)} collective-permute-done((bf16[512,512]{1,0:T(8,128)(2,1)S(1)}, bf16[512,512]{1,0:T(8,128)(2,1)}, u32[]{:S(2)}, u32[]{:S(2)}) %collective-permute-start.5) | collective-permute-done | bytes 524320 | tf_op jit(solution)/shard_map/ppermute | solution.py:16
  145.7 2.5 copy-done.4
  149.4 4.2 %shard_map.94 = (bf16[512,512]{1,0:T(8,128)(2,1)S(1)}, bf16[512,512]{1,0:T(8,128)(2,1)S(1)}, f32[8,512]{1,0:T(8,128)S(1)}, f32[8,256]{1,0:T(8,128)S(1)}) custom-call(bf16[512,512]{1,0:T(8,128)(2,1)S(1)} %broadcast_select_fusion.g_ref, f32[512,512]{1,0:T(8,128)S(1)} %copy-done.15, f32[8,256]{1,0:T(8,128)S(1)} %get-tuple-element.35.sq_ref, ...), custom_call_target="tpu_custom_call" | custom-call | flops 2415919104 | bytes 9000000 | tf_op jit(solution)/shard_map/pallas_call | solution.py:241
  156.0 4.6 %shard_map.95 = bf16[5120,512]{1,0:T(8,128)(2,1)S(1)} custom-call(bf16[512,512]{1,0:T(8,128)(2,1)S(1)} %broadcast_select_fusion.8.x_ref, bf16[512,512]{1,0:T(8,128)(2,1)S(1)} %get-tuple-element.42.dm_ref, bf16[512,512]{1,0:T(8,128)(2,1)S(1)} %pad_maximum_fusion.1.tail_ref), custom_call_target="tpu_custom_call" | custom-call | flops 2415919104 | bytes 7000000 | tf_op jit(solution)/shard_map/pallas_call | solution.py:292
  160.6 2.4 copy-done.5
  163.9 1.6 collective-permute-start.9
  168.4 4.5 %collective-permute-done.9 = bf16[320,512]{1,0:T(8,128)(2,1)S(1)} collective-permute-done((bf16[320,512]{1,0:T(8,128)(2,1)}, bf16[320,512]{1,0:T(8,128)(2,1)S(1)}, u32[]{:S(2)}, u32[]{:S(2)}) %collective-permute-start.9) | collective-permute-done | bytes 327712 | tf_op jit(solution)/shard_map/ppermute | solution.py:421
  174.4 2.2 add_convert_fusion.11
  176.5 1.7 collective-permute-start.10
  178.6 2.5 copy-done.10
  181.0 4.9 %shard_map.96 = (bf16[512,512]{1,0:T(8,128)(2,1)S(1)}, f32[512,512]{1,0:T(8,128)}, f32[8,512]{1,0:T(8,128)}, f32[8,256]{1,0:T(8,128)}, f32[8,256]{1,0:T(8,128)}, /*index=5*/f32[8,512]{1,0:T(8,128)}) custom-call(bf16[512,512]{1,0:T(8,128)(2,1)S(1)} %bitcast.30, bf16[5120,512]{1,0:T(8,128)(2,1)S(1)} %copy-done.10, bf16[512,256]{1,0:T(8,128)(2,1)S(1)} %reshape.71.red_ref, ...), custom_call_target="tpu_custom_call" | custom-call | flops 2415919104 | bytes 8000000 | tf_op jit(solution)/shard_map/pallas_call | solution.py:161
  186.0 2.1 collective-permute-start.6
  188.0 2.3 add_convert_fusion.10
  190.3 1.7 collective-permute-start.11
  192.4 5.3 %collective-permute-done.11 = bf16[320,512]{1,0:T(8,128)(2,1)} collective-permute-done((bf16[320,512]{1,0:T(8,128)(2,1)}, bf16[320,512]{1,0:T(8,128)(2,1)}, u32[]{:S(2)}, u32[]{:S(2)}) %collective-permute-start.11) | collective-permute-done | bytes 327712 | tf_op jit(solution)/shard_map/ppermute | solution.py:421
  197.7 1.7 collective-permute-done.18
  199.4 2.3 add_convert_fusion.9
  202.0 1.7 collective-permute-start.19
  203.7 2.5 copy-done.11
  206.2 4.9 %shard_map.97 = (bf16[512,512]{1,0:T(8,128)(2,1)S(1)}, f32[512,512]{1,0:T(8,128)}, f32[8,512]{1,0:T(8,128)}, f32[8,256]{1,0:T(8,128)}, f32[8,256]{1,0:T(8,128)}, /*index=5*/f32[8,512]{1,0:T(8,128)}) custom-call(bf16[512,512]{1,0:T(8,128)(2,1)S(1)} %broadcast_select_fusion.1.x_ref, bf16[5120,512]{1,0:T(8,128)(2,1)S(1)} %copy-done.11, ...), custom_call_target="tpu_custom_call" | custom-call | flops 2415919104 | bytes 8000000 | tf_op jit(solution)/shard_map/pallas_call | solution.py:161
  211.1 1.4 collective-permute-start.7
  212.6 2.3 add_convert_fusion.8
  215.2 1.7 collective-permute-start.20
  217.0 5.3 %collective-permute-done.13 = bf16[320,512]{1,0:T(8,128)(2,1)} collective-permute-done((bf16[320,512]{1,0:T(8,128)(2,1)}, bf16[320,512]{1,0:T(8,128)(2,1)}, u32[]{:S(2)}, u32[]{:S(2)}) %collective-permute-start.13) | collective-permute-done | bytes 327712 | tf_op jit(solution)/shard_map/ppermute | solution.py:421
  223.0 2.3 add_convert_fusion.7
  227.3 2.5 copy-done.12
  229.8 4.9 %shard_map.98 = (bf16[512,512]{1,0:T(8,128)(2,1)S(1)}, f32[512,512]{1,0:T(8,128)}, f32[8,512]{1,0:T(8,128)}, f32[8,256]{1,0:T(8,128)}, f32[8,256]{1,0:T(8,128)}, /*index=5*/f32[8,512]{1,0:T(8,128)}) custom-call(bf16[512,512]{1,0:T(8,128)(2,1)S(1)} %broadcast_select_fusion.4.x_ref, bf16[5120,512]{1,0:T(8,128)(2,1)S(1)} %copy-done.12, ...), custom_call_target="tpu_custom_call" | custom-call | flops 2415919104 | bytes 8000000 | tf_op jit(solution)/shard_map/pallas_call | solution.py:161
  234.7 1.4 collective-permute-start.8
  237.1 1.4 add_convert_fusion.6
  240.7 2.5 copy-done.13
  243.2 4.9 %shard_map.99 = (bf16[512,512]{1,0:T(8,128)(2,1)S(1)}, f32[512,512]{1,0:T(8,128)}, f32[8,512]{1,0:T(8,128)}, f32[8,256]{1,0:T(8,128)}, f32[8,256]{1,0:T(8,128)}, /*index=5*/f32[8,512]{1,0:T(8,128)}) custom-call(bf16[512,512]{1,0:T(8,128)(2,1)S(1)} %broadcast_select_fusion.7.x_ref, bf16[5120,512]{1,0:T(8,128)(2,1)S(1)} %copy-done.13, ...), custom_call_target="tpu_custom_call" | custom-call | flops 2415919104 | bytes 8000000 | tf_op jit(solution)/shard_map/pallas_call | solution.py:161
  250.4 2.1 shard_map.100
  (83 shorter events, 28.7 us)
Async XLA Ops:
  7.2 57.5 %copy-start.6 = (f32[1,327680]{1,0:T(1,128)S(1)}, f32[1,327680]{1,0:T(1,128)}, u32[]{:S(2)}) copy-start(f32[1,327680]{1,0:T(1,128)} %param.9) | copy-start | bytes 3932164
  7.2 148.8 %all-gather.2.cloned.1.call-start = ((), (), s32[]{:S(2)}) async-start(), calls=%async_computation | async-start | bytes 5898240 | tf_op jit(solution)/shard_map/all_gather | solution.py:454
  7.2 1.4 copy-start.7
  8.6 57.0 %copy-start.16 = (bf16[4,2,8,8,512]{4,3,2,1,0:T(8,128)(2,1)S(1)}, bf16[4,2,8,8,512]{4,3,2,1,0:T(8,128)(2,1)}, u32[]{:S(2)}) copy-start(bf16[4,2,8,8,512]{4,3,2,1,0:T(8,128)(2,1)} %param.5) | copy-start | bytes 1572868
  8.8 0.8 copy-start.9
  67.1 2.5 copy-start
  74.5 2.8 %collective-permute-start = (bf16[512,512]{1,0:T(8,128)(2,1)S(1)}, bf16[512,512]{1,0:T(8,128)(2,1)S(1)}, u32[]{:S(2)}, u32[]{:S(2)}) collective-permute-start(bf16[512,512]{1,0:T(8,128)(2,1)S(1)} %get-tuple-element.31), channel_id=1, source_target_pairs={{0,8},{1,9},{2,10},{3,11},{4,12},{5,13},{6,14},{7,15}} | collective-permute-start | bytes 1572872 | tf_op jit(solution)/shard_map/ppermute | solution.py:16
  77.4 2.5 copy-start.1
  84.9 1.4 collective-permute-start.1
  86.4 2.5 copy-start.2
  93.8 2.8 %collective-permute-start.2 = (bf16[512,512]{1,0:T(8,128)(2,1)S(1)}, bf16[512,512]{1,0:T(8,128)(2,1)}, u32[]{:S(2)}, u32[]{:S(2)}) collective-permute-start(bf16[512,512]{1,0:T(8,128)(2,1)S(1)} %get-tuple-element.33), channel_id=1, source_target_pairs={{16,24},{17,25},{18,26},{19,27},{20,28},{21,29},{22,30},{23,31}} | collective-permute-start | bytes 1572872 | tf_op jit(solution)/shard_map/ppermute | solution.py:16
  96.6 2.5 copy-start.3
  103.8 11.8 %copy-start.14 = (f32[512,512]{1,0:T(8,128)}, f32[512,512]{1,0:T(8,128)S(1)}, u32[]{:S(2)}) copy-start(f32[512,512]{1,0:T(8,128)S(1)} %get-tuple-element.34.mixed_ref) | copy-start | bytes 3145732
  108.9 0.7 collective-permute-start.3
  114.7 0.9 collective-permute-start.4
  120.7 23.8 %collective-permute-start.5 = (bf16[512,512]{1,0:T(8,128)(2,1)S(1)}, bf16[512,512]{1,0:T(8,128)(2,1)}, u32[]{:S(2)}, u32[]{:S(2)}) collective-permute-start(bf16[512,512]{1,0:T(8,128)(2,1)S(1)} %get-tuple-element.39), channel_id=1, source_target_pairs={{8,0},{9,1},{10,2},{11,3},{12,4},{13,5},{14,6},{15,7}} | collective-permute-start | bytes 1572872 | tf_op jit(solution)/shard_map/ppermute | solution.py:16
  145.6 2.5 copy-start.4
  148.1 1.2 copy-start.15
  160.6 2.4 copy-start.5
  163.9 9.1 %collective-permute-start.9 = (bf16[320,512]{1,0:T(8,128)(2,1)}, bf16[320,512]{1,0:T(8,128)(2,1)S(1)}, u32[]{:S(2)}, u32[]{:S(2)}) collective-permute-start(bf16[320,512]{1,0:T(8,128)(2,1)} %get-tuple-element.70), channel_id=1, source_target_pairs={{0,2},{2,4},{4,6},{6,7},{7,5},{5,3},{3,1},{1,0},{8,10},{10,12},{12... | collective-permute-start | bytes 983048 | tf_op jit(solution)/shard_map/ppermute | solution.py:421
  165.5 8.9 %collective-permute-start.16 = (bf16[320,512]{1,0:T(8,128)(2,1)}, bf16[320,512]{1,0:T(8,128)(2,1)}, u32[]{:S(2)}, u32[]{:S(2)}) collective-permute-start(bf16[320,512]{1,0:T(8,128)(2,1)} %get-tuple-element.71), channel_id=1, source_target_pairs={{2,0},{4,2},{6,4},{7,6},{5,7},{3,5},{1,3},{0,1},{10,8},{12,10},{14... | collective-permute-start | bytes 983048 | tf_op jit(solution)/shard_map/ppermute | solution.py:421
  176.5 11.5 %collective-permute-start.10 = (bf16[320,512]{1,0:T(8,128)(2,1)}, bf16[320,512]{1,0:T(8,128)(2,1)}, u32[]{:S(2)}, u32[]{:S(2)}) collective-permute-start(bf16[320,512]{1,0:T(8,128)(2,1)} %get-tuple-element.68), channel_id=1, source_target_pairs={{0,2},{2,4},{4,6},{6,7},{7,5},{5,3},{3,1},{1,0},{8,10},{10,12},{12... | collective-permute-start | bytes 983048 | tf_op jit(solution)/shard_map/ppermute | solution.py:421
  178.3 9.8 %collective-permute-start.17 = (bf16[320,512]{1,0:T(8,128)(2,1)}, bf16[320,512]{1,0:T(8,128)(2,1)}, u32[]{:S(2)}, u32[]{:S(2)}) collective-permute-start(bf16[320,512]{1,0:T(8,128)(2,1)} %get-tuple-element.69), channel_id=1, source_target_pairs={{2,0},{4,2},{6,4},{7,6},{5,7},{3,5},{1,3},{0,1},{10,8},{12,10},{14... | collective-permute-start | bytes 983048 | tf_op jit(solution)/shard_map/ppermute | solution.py:421
  178.6 2.5 copy-start.10
  186.0 6.4 %collective-permute-start.6 = (bf16[512,512]{1,0:T(8,128)(2,1)S(1)}, bf16[512,512]{1,0:T(8,128)(2,1)}, u32[]{:S(2)}, u32[]{:S(2)}) collective-permute-start(bf16[512,512]{1,0:T(8,128)(2,1)S(1)} %get-tuple-element.49), channel_id=1, source_target_pairs={{0,8},{1,9},{2,10},{3,11},{4,12},{5,13},{6,14},{7,15}} | collective-permute-start | bytes 1572872 | tf_op jit(solution)/shard_map/ppermute | solution.py:16
  190.3 7.4 %collective-permute-start.11 = (bf16[320,512]{1,0:T(8,128)(2,1)}, bf16[320,512]{1,0:T(8,128)(2,1)}, u32[]{:S(2)}, u32[]{:S(2)}) collective-permute-start(bf16[320,512]{1,0:T(8,128)(2,1)} %get-tuple-element.66), channel_id=1, source_target_pairs={{0,2},{2,4},{4,6},{6,7},{7,5},{5,3},{3,1},{1,0},{8,10},{10,12},{12... | collective-permute-start | bytes 983048 | tf_op jit(solution)/shard_map/ppermute | solution.py:421
  192.1 7.4 %collective-permute-start.18 = (bf16[320,512]{1,0:T(8,128)(2,1)}, bf16[320,512]{1,0:T(8,128)(2,1)}, u32[]{:S(2)}, u32[]{:S(2)}) collective-permute-start(bf16[320,512]{1,0:T(8,128)(2,1)} %get-tuple-element.67), channel_id=1, source_target_pairs={{2,0},{4,2},{6,4},{7,6},{5,7},{3,5},{1,3},{0,1},{10,8},{12,10},{14... | collective-permute-start | bytes 983048 | tf_op jit(solution)/shard_map/ppermute | solution.py:421
  201.7 10.9 %collective-permute-start.12 = (bf16[320,512]{1,0:T(8,128)(2,1)}, bf16[320,512]{1,0:T(8,128)(2,1)}, u32[]{:S(2)}, u32[]{:S(2)}) collective-permute-start(bf16[320,512]{1,0:T(8,128)(2,1)} %get-tuple-element.64), channel_id=1, source_target_pairs={{0,2},{2,4},{4,6},{6,7},{7,5},{5,3},{3,1},{1,0},{8,10},{10,12},{12... | collective-permute-start | bytes 983048 | tf_op jit(solution)/shard_map/ppermute | solution.py:421
  202.0 10.6 %collective-permute-start.19 = (bf16[320,512]{1,0:T(8,128)(2,1)}, bf16[320,512]{1,0:T(8,128)(2,1)}, u32[]{:S(2)}, u32[]{:S(2)}) collective-permute-start(bf16[320,512]{1,0:T(8,128)(2,1)} %get-tuple-element.65), channel_id=1, source_target_pairs={{2,0},{4,2},{6,4},{7,6},{5,7},{3,5},{1,3},{0,1},{10,8},{12,10},{14... | collective-permute-start | bytes 983048 | tf_op jit(solution)/shard_map/ppermute | solution.py:421
  203.7 2.5 copy-start.11
  211.1 5.8 %collective-permute-start.7 = (bf16[512,512]{1,0:T(8,128)(2,1)S(1)}, bf16[512,512]{1,0:T(8,128)(2,1)}, u32[]{:S(2)}, u32[]{:S(2)}) collective-permute-start(bf16[512,512]{1,0:T(8,128)(2,1)S(1)} %get-tuple-element.50), channel_id=1, source_target_pairs={{8,16},{9,17},{10,18},{11,19},{12,20},{13,21},{14,22},{15,23}} | collective-permute-start | bytes 1572872 | tf_op jit(solution)/shard_map/ppermute | solution.py:16
  214.9 7.4 %collective-permute-start.13 = (bf16[320,512]{1,0:T(8,128)(2,1)}, bf16[320,512]{1,0:T(8,128)(2,1)}, u32[]{:S(2)}, u32[]{:S(2)}) collective-permute-start(bf16[320,512]{1,0:T(8,128)(2,1)} %get-tuple-element.62), channel_id=1, source_target_pairs={{0,2},{2,4},{4,6},{6,7},{7,5},{5,3},{3,1},{1,0},{8,10},{10,12},{12... | collective-permute-start | bytes 983048 | tf_op jit(solution)/shard_map/ppermute | solution.py:421
  215.2 7.8 %collective-permute-start.20 = (bf16[320,512]{1,0:T(8,128)(2,1)}, bf16[320,512]{1,0:T(8,128)(2,1)}, u32[]{:S(2)}, u32[]{:S(2)}) collective-permute-start(bf16[320,512]{1,0:T(8,128)(2,1)} %get-tuple-element.63), channel_id=1, source_target_pairs={{2,0},{4,2},{6,4},{7,6},{5,7},{3,5},{1,3},{0,1},{10,8},{12,10},{14... | collective-permute-start | bytes 983048 | tf_op jit(solution)/shard_map/ppermute | solution.py:421
  225.3 11.8 %collective-permute-start.14 = (bf16[320,512]{1,0:T(8,128)(2,1)}, bf16[320,512]{1,0:T(8,128)(2,1)}, u32[]{:S(2)}, u32[]{:S(2)}) collective-permute-start(bf16[320,512]{1,0:T(8,128)(2,1)} %get-tuple-element.60), channel_id=1, source_target_pairs={{0,2},{2,4},{4,6},{6,7},{7,5},{5,3},{3,1},{1,0},{8,10},{10,12},{12... | collective-permute-start | bytes 983048 | tf_op jit(solution)/shard_map/ppermute | solution.py:421
  226.6 10.5 %collective-permute-start.21 = (bf16[320,512]{1,0:T(8,128)(2,1)}, bf16[320,512]{1,0:T(8,128)(2,1)}, u32[]{:S(2)}, u32[]{:S(2)}) collective-permute-start(bf16[320,512]{1,0:T(8,128)(2,1)} %get-tuple-element.61), channel_id=1, source_target_pairs={{2,0},{4,2},{6,4},{7,6},{5,7},{3,5},{1,3},{0,1},{10,8},{12,10},{14... | collective-permute-start | bytes 983048 | tf_op jit(solution)/shard_map/ppermute | solution.py:421
  227.3 2.5 copy-start.12
  234.7 5.9 %collective-permute-start.8 = (bf16[512,512]{1,0:T(8,128)(2,1)S(1)}, bf16[512,512]{1,0:T(8,128)(2,1)}, u32[]{:S(2)}, u32[]{:S(2)}) collective-permute-start(bf16[512,512]{1,0:T(8,128)(2,1)S(1)} %get-tuple-element.51), channel_id=1, source_target_pairs={{16,24},{17,25},{18,26},{19,27},{20,28},{21,29},{22,30},{23,31}} | collective-permute-start | bytes 1572872 | tf_op jit(solution)/shard_map/ppermute | solution.py:16
  238.5 10.5 %collective-permute-start.15 = (bf16[320,512]{1,0:T(8,128)(2,1)S(1)}, bf16[320,512]{1,0:T(8,128)(2,1)S(1)}, u32[]{:S(2)}, u32[]{:S(2)}) collective-permute-start(bf16[320,512]{1,0:T(8,128)(2,1)S(1)} %get-tuple-element.58), channel_id=1, source_target_pairs={{0,2},{2,4},{4,6},{6,7},{7,5},{5,3},{3,1},{1,0},{8,10},{10,12},{12... | collective-permute-start | bytes 983048 | tf_op jit(solution)/shard_map/ppermute | solution.py:421
  239.9 9.1 %collective-permute-start.22 = (bf16[320,512]{1,0:T(8,128)(2,1)S(1)}, bf16[320,512]{1,0:T(8,128)(2,1)S(1)}, u32[]{:S(2)}, u32[]{:S(2)}) collective-permute-start(bf16[320,512]{1,0:T(8,128)(2,1)S(1)} %get-tuple-element.59), channel_id=1, source_target_pairs={{2,0},{4,2},{6,4},{7,6},{5,7},{3,5},{1,3},{0,1},{10,8},{12,10},{14... | collective-permute-start | bytes 983048 | tf_op jit(solution)/shard_map/ppermute | solution.py:421
  240.7 2.5 copy-start.13
  248.1 2.3 copy-start.8
Sparse Core Ops, SparseCore 0:
  65.8 86.3 all-gather.1
